TPU v7x, 32 devices: a whole 2x2x4 slice. The times are simulated.
32 devices in a mesh: dp: 8 (over z, x), tensor: 4 (over y, core).
Axes of the slice: x: 2, y: 2, z: 4, core: 2. Of those that a mesh axis runs over, the one named last changes fastest.
Arguments:
- inputs: bfloat16 [24, 1024, 512], P('dp', 'tensor'), may hold values from -6 to 6
- cotangent: bfloat16 [24, 1024, 512], P('dp', 'tensor'), may hold values from -6 to 6
- mix_weight: bfloat16 [512, 1536], P(('dp', 'tensor')), may hold values from -0.25 to 0.25
- gate_weight: bfloat16 [512, 8], P(('dp', 'tensor')), may hold values from -0.25 to 0.25
- gate_bias: float32 [8], replicated, may hold values from 2.5 to 8
- out_weight: bfloat16 [512, 512], P(('dp', 'tensor')), may hold values from -1 to 1
- gain_first: bfloat16 [512], P(('dp', 'tensor')), may hold values from 0.5 to 1.5
- shift_first: bfloat16 [512], P(('dp', 'tensor')), may hold values from -2.5 to 2.5
- gain_second: bfloat16 [512], P(('dp', 'tensor')), may hold values from 0.5 to 1.5
- shift_second: bfloat16 [512], P(('dp', 'tensor')), may hold values from -2.5 to 2.5
- up_weight: bfloat16 [512, 2048], P('dp', 'tensor'), may hold values from -0.25 to 0.25
- down_weight: bfloat16 [2048, 512], P('tensor', 'dp'), may hold values from -0.125 to 0.125
- random_maps: bfloat16 [8, 64, 64], replicated, may hold values from -0.75 to 0.75
Outputs:
- output: bfloat16 [24, 1024, 512], P('dp', 'tensor')
- input_grad: float32 [24, 1024, 512], P('dp', 'tensor')
- mix_grad: float32 [512, 1536], P(('dp', 'tensor'))
- gate_grad: float32 [512, 8], P(('dp', 'tensor'))
- bias_grad: float32 [8], replicated
- out_grad: float32 [512, 512], P(('dp', 'tensor'))
- first_gain_grad: float32 [512], P(('dp', 'tensor'))
- first_shift_grad: float32 [512], P(('dp', 'tensor'))
- second_gain_grad: float32 [512], P(('dp', 'tensor'))
- second_shift_grad: float32 [512], P(('dp', 'tensor'))
- up_grad: float32 [512, 2048], P('dp', 'tensor')
- down_grad: float32 [2048, 512], P('tensor', 'dp')
All inputs are finite; a program needn't handle non-finite values.
Results may differ from a plain program's by a relative error of at most 0.012.
Values may be sent and summed in bfloat16 or wider, within the bound.
No kernel may reach another device: no remote copies, remote signals or barrier semaphores. Data moves between devices by JAX's collectives and lax.ppermute only.
A program may use at most 192 MiB of HBM per device.

v0:
```python
import functools

import jax
import jax.numpy as jnp
from jax import lax
from jax.experimental import pallas as pl
from jax.experimental.pallas import tpu as pltpu
from jax.sharding import PartitionSpec as P

BOTH = ("dp", "tensor")
F32 = jnp.float32
BF16 = jnp.bfloat16
EPSILON = 1e-05
DENSITY = 0.3989422804014327
SIN = (9.9999999998e-01, -1.6666666617e-01, 8.3333309689e-03, -1.9840860382e-04, 2.7525224003e-06, -2.3888330913e-08)
COS = (9.9999999978e-01, -4.9999999354e-01, 4.1666636104e-02, -1.3888359409e-03, 2.4760057595e-05, -2.6049626765e-07)

NN = (((1,), (0,)), ((), ()))
NT = (((1,), (1,)), ((), ()))
TN = (((0,), (0,)), ((), ()))


def mm(a, b, dims=NN):
    return lax.dot_general(a, b, dims, preferred_element_type=F32)


def low(a):
    return a.astype(BF16)


def lanes_of(shape):
    return lax.broadcasted_iota(jnp.int32, shape, len(shape) - 1)


def swap_halves(a):
    return pltpu.roll(a, 64, 1)


def sincos(a):
    turns = jnp.floor(a * 0.3183098861837907 + 0.5)
    r = (a - turns * 3.140625) - turns * 9.676535897932e-4
    half = turns * 0.5
    sign = 1.0 - 4.0 * (half - jnp.floor(half))
    r2 = r * r
    s = r * (SIN[0] + r2 * (SIN[1] + r2 * (SIN[2] + r2 * (SIN[3] + r2 * (SIN[4] + r2 * SIN[5])))))
    c = COS[0] + r2 * (COS[1] + r2 * (COS[2] + r2 * (COS[3] + r2 * (COS[4] + r2 * COS[5]))))
    return sign * s, sign * c


def normal_parts(v):
    t = pl.reciprocal(1.0 + 0.23164189 * jnp.abs(v), approx=True)
    bell = jnp.exp(-0.5 * (v * v))
    poly = t * (0.127414796 + t * (-0.142248368 + t * (0.7107068705 + t * (-0.7265760135 + t * 0.5307027145))))
    tail = poly * bell
    return jnp.where(v >= 0.0, 1.0 - tail, tail), DENSITY * bell


def three_parts(a):
    high = a.astype(BF16)
    rest = a - high.astype(F32)
    mid = rest.astype(BF16)
    return high, mid, (rest - mid.astype(F32)).astype(BF16)


def tri_sum(tri, a):
    high, mid, rest = (part.astype(F32) for part in three_parts(a))
    packed = mm(tri, low(high + pltpu.roll(mid, 4, 1) + pltpu.roll(rest, 8, 1)))
    return packed + pltpu.roll(packed, 124, 1) + pltpu.roll(packed, 120, 1)


def norm_of(x):
    mean = jnp.mean(x, axis=-1, keepdims=True)
    centered = x - mean
    inv = lax.rsqrt(jnp.mean(centered * centered, axis=-1, keepdims=True) + EPSILON)
    return centered * inv, inv


def norm_back(s, unit, inv):
    return inv * (
        s
        - jnp.mean(s, axis=-1, keepdims=True)
        - unit * jnp.mean(s * unit, axis=-1, keepdims=True)
    )


def chip_row(pos, mz, mx, my):
    return (((pos[0] ^ mz) * 2 + (pos[1] ^ mx)) * 2 + (pos[2] ^ my)) * 32


def lower_tri(n):
    row = lax.broadcasted_iota(jnp.int32, (n, n), 0)
    col = lax.broadcasted_iota(jnp.int32, (n, n), 1)
    return row, col


def unpack_states(pack, b, zcols, last=65):
    lane = lanes_of((128, 128))
    out = []
    for p in range(2):
        both = pack[2 * b + p].astype(F32)
        for h, mat in ((2 * p, both), (2 * p + 1, swap_halves(both))):
            z = jnp.sum(jnp.where(lane == 4 * b + h, zcols, 0.0), axis=1, keepdims=True)
            out.append(jnp.where(lane < 64, mat, jnp.where(lane <= last, z, 0.0)))
    return out


def pack_states(states, pack_o, b, last, split=False):
    lane = lanes_of((128, 128))
    zcols = jnp.where(b == 0, 0.0, pack_o[last].astype(F32))

    def sum_of(s):
        return s[:, 64:65] + s[:, 65:66] if split else s[:, 64:65]

    for p in range(2):
        s0, s1 = states[2 * p], states[2 * p + 1]
        pack_o[2 * b + p] = jnp.where(lane < 64, s0, swap_halves(s1)).astype(BF16)
        zcols = jnp.where(lane == 4 * b + 2 * p, sum_of(s0), zcols)
        zcols = jnp.where(lane == 4 * b + 2 * p + 1, sum_of(s1), zcols)
    pack_o[last] = zcols.astype(BF16)


def pack_kernel(pos, mix, columns, keep_o, send_o):
    width = mix.shape[1] // 6
    rows = mix.shape[0]
    table = jnp.concatenate(
        [columns[...].astype(F32), jnp.zeros((128 - columns.shape[0], rows), F32)], axis=0
    )
    sides = jnp.concatenate([table, jnp.zeros((128, 128 - rows), F32)], axis=1).T[0:rows]
    lane = lanes_of(sides.shape)
    moved = pltpu.roll(sides, 124, 1)
    halves = []
    for s, block in ((0, jnp.where(lane < 4, sides, moved)), (1, moved)):
        parts = [mix[:, (2 * i + s) * width : (2 * i + s + 1) * width] for i in range(3)]
        halves.append(jnp.concatenate(parts + [low(jnp.where(lane < 8, block, 0.0))], axis=1))
    first = pos[3] == 0
    keep_o[...] = jnp.where(first, halves[0], halves[1])
    send_o[...] = jnp.where(first, halves[1], halves[0])


def prepare_kernel(b, pos, own, oth, cot, unit_o, cott_o):
    chunk = own.shape[1]
    first = pos[3] == 0
    mine, theirs = own[0], oth[0]
    for j in range(2):
        unit, _ = norm_of(jnp.where(first == (j == 0), mine, theirs).astype(F32))
        unit_o[0, j * chunk : (j + 1) * chunk] = unit
    cott_o[0] = low(cot[0].astype(F32).T)


def feature_parts(angles, lane):
    s, c = sincos(angles)
    out = []
    turned_s, turned_c = swap_halves(s), swap_halves(c)
    for f, turned in (
        (jnp.where(lane < 64, s, turned_c), jnp.where(lane < 64, c, turned_s)),
        (jnp.where(lane < 64, turned_s, c), jnp.where(lane < 64, turned_c, s)),
    ):
        high = low(f)
        out.append((high, low(f - high.astype(F32)), low(turned)))
    return out


def query_kernel(b, a, wmix, maps, fq_o, fql_o, fqt_o):
    chunk = a.shape[1] // 2
    lane = lanes_of((chunk, 128))
    spans = [slice(j * chunk, (j + 1) * chunk) for j in range(2)]
    mixed = [low(mm(a[0, rows], wmix[:, 0:256])) for rows in spans]
    angles = [[mm(m[:, 128 * p : 128 * p + 128], maps[p]) for p in range(2)] for m in mixed]
    for j, rows in enumerate(spans):
        for p in range(2):
            for i, (high, rest, turned) in enumerate(feature_parts(angles[j][p], lane)):
                fq_o[0, 2 * p + i, rows], fql_o[0, 2 * p + i, rows], fqt_o[0, 2 * p + i, rows] = high, rest, turned


def project_kernel(
    b, pos, units, w0, w1, w2, w3, bias, maps,
    a_o, fk_o, fkl_o, fkt_o, va_o, ccol_o, ucol_o, crow_o, smid_o, pack_o, wmix_o, vec_o, vbar_o,
    w_s, sems,
):
    chunk = units.shape[1] // 2

    @pl.when(b == 0)
    def _():
        copies = [
            pltpu.make_async_copy(piece, w_s.at[:, pos[1] ^ mx, pos[2] ^ my], sems.at[2 * my + mx])
            for piece, (my, mx) in ((w0, (0, 0)), (w1, (0, 1)), (w2, (1, 0)), (w3, (1, 1)))
        ]
        for copy in copies:
            copy.start()
        for copy in copies:
            copy.wait()
        wmix_o[...] = w_s[...].reshape(wmix_o.shape)
        vec_o[...] = wmix_o[:, 768:896].astype(F32).T[0:8]
        vbar_o[...] = mm(jnp.broadcast_to(vec_o[5:6], vec_o.shape).astype(BF16), wmix_o[:, 512:768])

    gain, shift = vec_o[4:5], vec_o[5:6]
    row, col = lower_tri(chunk)
    tri = jnp.where(row >= col, 1.0, 0.0).astype(BF16)
    lane = lanes_of((chunk, 128))
    spans = [slice(j * chunk, (j + 1) * chunk) for j in range(2)]
    attends = [low(units[0, rows] * gain + shift) for rows in spans]
    for a, rows in zip(attends, spans):
        a_o[0, rows] = a
    wide = [mm(a, wmix_o[:, 256:896]) for a in attends]
    mixed = [low(m[:, 0:512]) for m in wide]
    angles = [[mm(m[:, 128 * p : 128 * p + 128], maps[p]) for p in range(2)] for m in mixed]
    douts, ends = [], []
    for j, rows in enumerate(spans):
        logits = wide[j][:, 512:640] + bias[...]
        e = jnp.exp(-jnp.abs(logits))
        w = 1.0 + e
        log1 = jnp.where(w == 1.0, e, jnp.log(w) * (e / jnp.where(w == 1.0, 1.0, w - 1.0)))
        log_gate = jnp.where(lane < 4, jnp.minimum(logits, 0.0) - log1, 0.0)
        fresh = jnp.where(lane < 4, jnp.where(logits >= 0.0, e, 1.0) / w, 0.0)
        cum = jnp.where(lane < 4, tri_sum(tri, log_gate), 0.0)
        ccol_o[0, rows] = cum
        ucol_o[0, rows] = fresh
        crow_o[0, j] = (cum + pltpu.roll(fresh, 4, 1)).T[0:8]
        ends.append(cum[chunk - 1 : chunk])
        douts.append(jnp.exp(ends[j] - cum) * fresh)
    one = jnp.where((lane == 64) | (lane == 65), 1.0, 0.0)
    shares = [[None] * 4, [None] * 4]
    for j, rows in enumerate(spans):
        for p in range(2):
            v = mixed[j][:, 256 + 128 * p : 384 + 128 * p].astype(F32) - vbar_o[0:1, 128 * p : 128 * p + 128]
            for h, vh in ((2 * p, v), (2 * p + 1, swap_halves(v))):
                aug = jnp.where(lane < 64, vh, one)
                va_o[0, h, rows] = low(aug)
                shares[j][h] = low(aug * douts[j][:, h : h + 1])
    locals_ = [[None] * 4, [None] * 4]
    for j, rows in enumerate(spans):
        for p in range(2):
            parts = feature_parts(angles[j][p], lane)
            for h in (2 * p, 2 * p + 1):
                fk_o[0, h, rows], fkl_o[0, h, rows], fkt_o[0, h, rows] = parts[h - 2 * p]
                locals_[j][h] = mm(parts[h - 2 * p][0], shares[j][h], TN)
    states = []
    for h in range(4):
        smid_o[0, h] = locals_[0][h]
        states.append(locals_[0][h] * jnp.exp(ends[1][:, h : h + 1]) + locals_[1][h])
    pack_states(states, pack_o, b, pack_o.shape[0] - 1)


def weights_of(ccol, ucol_row, crow, row, col):
    gap = jnp.minimum(ccol - crow, 0.0)
    return jnp.where(row >= col, jnp.exp(gap), 0.0) * ucol_row


def pairs_of(chunk):
    return [(j, h, slice(j * chunk, (j + 1) * chunk)) for j in range(2) for h in range(4)]


def scores(fq, fk, fql, fkl, h, rows):
    q, k = fq[0, h, rows], fk[0, h, rows]
    return mm(
        jnp.concatenate([q, fql[0, h, rows], q], axis=1), jnp.concatenate([k, k, fkl[0, h, rows]], axis=1), NT
    )


def local_kernel(b, fq, fk, fql, fkl, va, ccol, crow, o_o):
    chunk = crow.shape[3]
    row, col = lower_tri(chunk)
    pairs = pairs_of(chunk)
    qk = [scores(fq, fk, fql, fkl, h, rows) for j, h, rows in pairs]
    attn = [
        low(q * weights_of(ccol[0, rows, h : h + 1], crow[0, j, 4 + h : 5 + h], crow[0, j, h : h + 1], row, col))
        for q, (j, h, rows) in zip(qk, pairs)
    ]
    outs = [mm(a, va[0, h, rows]) for a, (j, h, rows) in zip(attn, pairs)]
    for out, (j, h, rows) in zip(outs, pairs):
        o_o[0, h, rows] = out


def mean_of(vbar, h):
    pair = vbar[:, 128 * (h // 2) : 128 * (h // 2) + 128]
    return (pair if h % 2 == 0 else swap_halves(pair))[0:1]


def finish_kernel(b, pos, o_loc, fq, ccol, pack, smid, vbar, inv_o, turn_o, st_o, keep_o, send_o):
    chunk = ccol.shape[1] // 2
    zcols = pack[pack.shape[0] - 1].astype(F32)
    states = unpack_states(pack, b, zcols)
    lane = lanes_of((chunk, 128))
    cend = ccol[0, chunk - 1 : chunk]
    pairs = pairs_of(chunk)
    near = []
    for h in range(4):
        near.append(low(states[h]))
        near.append(low(jnp.exp(cend[:, h : h + 1]) * states[h] + smid[0, h]))
        for j in range(2):
            st_o[0, h, j] = near[2 * h + j]
    inter = [mm(fq[0, h, rows], near[2 * h + j]) for j, h, rows in pairs]
    outs = [
        o_loc[0, h, rows] + jnp.exp(ccol[0, rows, h : h + 1]) * part for part, (j, h, rows) in zip(inter, pairs)
    ]
    dens = [jnp.broadcast_to(o[:, 64:65], o.shape) for o in outs]
    invs = [lax.rsqrt(den * den + 1.0) for den in dens]
    att = [[None] * 4, [None] * 4]
    for o, den, inv, (j, h, rows) in zip(outs, dens, invs, pairs):
        mean = mean_of(vbar, h)
        att[j][h] = (o + den * mean) * inv
        inv_o[0, h, rows] = jnp.where(lane < 64, inv, 0.0)
        turn_o[0, h, rows] = mean - den * inv * att[j][h]
    first = pos[3] == 0
    for p in range(2):
        both = [
            jnp.where(lane < 64, att[j][2 * p], swap_halves(att[j][2 * p + 1])) for j in range(2)
        ]
        keep_o[0, :, 128 * p : 128 * p + 128] = jnp.where(first, both[0], both[1]).astype(BF16)
        send_o[0, :, 128 * p : 128 * p + 128] = jnp.where(first, both[1], both[0]).astype(BF16)


def dp_of(pos, mz, mx):
    return (pos[0] ^ mz) * 2 + (pos[1] ^ mx)


def feed_chunks(pos, near, far, cot, cott, feed, feedt, target, up_s, dn_s, hid_s, gp_s, big_s):
    seqs, chunk, _ = cot.shape
    nz = far.shape[0]
    width, both = up_s.shape
    hidden = both // 2
    rows_up = width // (2 * nz)
    for my in range(2):
        cols = slice(my * hidden, (my + 1) * hidden)
        for mx in range(2):
            k = 2 * my + mx
            piece = far if k == 3 else near.at[pl.ds(k * nz, nz)]
            for z in range(nz):
                at = pl.multiple_of((2 * z + (pos[1] ^ mx)) * rows_up, rows_up)
                up_s[pl.ds(at, rows_up), cols] = piece[z, 0:rows_up]
                dn_s[pl.ds(at, rows_up), cols] = piece[z, rows_up : 2 * rows_up]

    def scatter(offset):
        for my in range(2):
            cols = slice(my * hidden, (my + 1) * hidden)
            for mx in range(2):
                for mz in range(nz):
                    at = pl.multiple_of(dp_of(pos, mz, mx) * rows_up, rows_up)
                    target[my, mx, mz, offset : offset + rows_up, :] = big_s[pl.ds(at, rows_up), cols]

    spans = [slice(r * chunk, (r + 1) * chunk) for r in range(seqs)]
    outs, grads = [], []
    pres = [mm(feed[rows], up_s[...]) for rows in spans]
    ghs = [mm(cot[r], dn_s[...]) for r in range(seqs)]
    for r, rows in enumerate(spans):
        cdf, pdf = normal_parts(pres[r])
        hid_s[rows] = low(pres[r] * cdf)
        gp_s[rows] = low(ghs[r] * (cdf + pres[r] * pdf))
    for rows in spans:
        outs.append(mm(hid_s[rows], dn_s[...], NT))
        grads.append(mm(gp_s[rows], up_s[...], NT))
    big_s[...] = low(mm(feedt[...], gp_s[...]))
    scatter(0)
    big_s[...] = low(mm(jnp.concatenate([cott[r] for r in range(seqs)], axis=1), hid_s[...]))
    scatter(rows_up)
    return outs, grads


def feed_first_kernel(
    pos, akeep, arecv, x, cot, cott, vec, near_own, far_own, near, far,
    gsend_o, acc_o, gf_o, mid_o, feed_o, feedt_o, att_o, ow_o,
    up_s, dn_s, hid_s, gp_s, big_s,
):
    seqs, chunk, _ = x.shape
    nz = far.shape[0]
    rows_up = up_s.shape[0] // (2 * nz)
    first = pos[3] == 0
    for mc, (some, rest) in enumerate(((near_own, far_own), (near, far))):
        for my in range(2):
            t = (pos[2] ^ my) * 2 + (pos[3] ^ mc)
            for mx in range(2):
                k = 2 * my + mx
                for z in range(nz):
                    at = pl.multiple_of(((2 * z + (pos[1] ^ mx)) * 4 + t) * 16, 16)
                    source = rest if k == 3 else some.at[pl.ds(k * nz, nz)]
                    ow_o[pl.ds(at, 16), :] = source[z, 2 * rows_up :]
    gain, shift = vec[6:7], vec[7:8]
    for r in range(seqs):
        rows = slice(r * chunk, (r + 1) * chunk)
        mine, theirs = akeep[r], arecv[r]
        att = jnp.concatenate([jnp.where(first, mine, theirs), jnp.where(first, theirs, mine)], axis=1)
        att_o[rows] = att
        mid = x[r].astype(F32) + mm(att, ow_o[...])
        mid_o[rows] = mid
        unit, _ = norm_of(mid)
        feed = unit * gain + shift
        feed_o[rows] = low(feed)
        feedt_o[:, rows] = low(feed.T)
    outs, grads = feed_chunks(pos, near, far, cot, cott, feed_o, feedt_o, gsend_o, up_s, dn_s, hid_s, gp_s, big_s)
    for r, (out, grad) in enumerate(zip(outs, grads)):
        acc_o[r * chunk : (r + 1) * chunk] = out
        gf_o[r * chunk : (r + 1) * chunk] = grad


def feed_second_kernel(
    pos, cot, cott, vec, near, far, acc, gf_in, mid_in, feed, feedt, att, ow,
    out_o, gm_o, gak_o, gas_o, gkeep_o, okeep_o, osend_o, gv_o,
    up_s, dn_s, hid_s, gp_s, gb_s, big_s,
):
    seqs, chunk, width = cot.shape
    nz = far.shape[0]
    first = pos[3] == 0
    outs, grads = feed_chunks(pos, near, far, cot, cott, feed, feedt, gkeep_o, up_s, dn_s, hid_s, gp_s, big_s)
    gain = vec[6:7]
    gain_sum = jnp.zeros((1, width), F32)
    shift_sum = jnp.zeros((1, width), F32)
    for r in range(seqs):
        rows = slice(r * chunk, (r + 1) * chunk)
        mid = mid_in[rows]
        out_o[r] = low(mid + (acc[rows] + outs[r]))
        unit, inv = norm_of(mid)
        gf = gf_in[rows] + grads[r]
        gain_sum += jnp.sum(gf * unit, axis=0, keepdims=True)
        shift_sum += jnp.sum(gf, axis=0, keepdims=True)
        gm = cot[r].astype(F32) + norm_back(gf * gain, unit, inv)
        gm_o[r] = gm
        gb = low(gm)
        gb_s[rows] = gb
        ga = low(mm(gb, ow[...], NT))
        half = width // 2
        gak_o[r] = jnp.where(first, ga[:, :half], ga[:, half:])
        gas_o[r] = jnp.where(first, ga[:, half:], ga[:, :half])
    gv_o[...] = jnp.concatenate([gain_sum, shift_sum, jnp.zeros((6, width), F32)], axis=0)
    big_s[:, 0:width] = low(mm(att[...], gb_s[...], TN))
    for mc, target in ((0, okeep_o), (1, osend_o)):
        for my in range(2):
            t = (pos[2] ^ my) * 2 + (pos[3] ^ mc)
            for mx in range(2):
                for mz in range(nz):
                    at = pl.multiple_of((dp_of(pos, mz, mx) * 4 + t) * 16, 16)
                    target[my, mx, mz] = big_s[pl.ds(at, 16), 0:width]


def adjoint_kernel(b, pos, gak, gar, inv_root, turn, fq, ccol, g_o, scaled_o, l1_o, pack_o):
    chunk = ccol.shape[1] // 2
    lane = lanes_of((chunk, 128))
    first = pos[3] == 0
    pairs = pairs_of(chunk)
    gas = []
    for j in range(2):
        for p in range(2):
            cols = slice(128 * p, 128 * p + 128)
            pair = jnp.where(first == (j == 0), gak[0, :, cols], gar[0, :, cols]).astype(F32)
            gas += [pair, swap_halves(pair)]
    gns = [low(ga * inv_root[0, h, rows]).astype(F32) for ga, (j, h, rows) in zip(gas, pairs)]
    gds = [
        jnp.sum(gn * turn[0, h, rows], axis=1, keepdims=True) for gn, (j, h, rows) in zip(gns, pairs)
    ]
    scaled = []
    for gn, gd, (j, h, rows) in zip(gns, gds, pairs):
        gd = jnp.broadcast_to(gd, gn.shape)
        high = low(gd).astype(F32)
        g = jnp.where(lane == 64, high, jnp.where(lane == 65, gd - high, gn))
        g_o[0, h, rows] = low(g)
        scaled.append(low(g * jnp.exp(ccol[0, rows, h : h + 1])))
        scaled_o[0, h, rows] = scaled[-1]
    parts = [mm(fq[0, h, rows], g, TN) for g, (j, h, rows) in zip(scaled, pairs)]
    states = []
    for h in range(4):
        l1_o[0, h] = parts[4 + h]
        states.append(parts[h] + jnp.exp(ccol[0, chunk - 1 : chunk, h : h + 1]) * parts[4 + h])
    pack_states(states, pack_o, b, pack_o.shape[0] - 1, split=True)


def local_back_kernel(b, fq, fk, va, g, scaled, st, ccol, crow, dfq_o, dfk_o, dva_o):
    chunk = crow.shape[3]
    row, col = lower_tri(chunk)
    pairs = pairs_of(chunk)
    for half in (pairs[:4], pairs[4:]):
        qk = [mm(fq[0, h, rows], fk[0, h, rows], NT) for j, h, rows in half]
        da = [mm(g[0, h, rows], va[0, h, rows], NT) for j, h, rows in half]
        inter = [mm(scaled[0, h, rows], st[0, h, j], NT) for j, h, rows in half]
        attn, dp = [], []
        for q, d, (j, h, rows) in zip(qk, da, half):
            w = weights_of(ccol[0, rows, h : h + 1], crow[0, j, 4 + h : 5 + h], crow[0, j, h : h + 1], row, col)
            attn.append(low(q * w))
            dp.append(low(d * w))
        dva = [mm(a, g[0, h, rows], TN) for a, (j, h, rows) in zip(attn, half)]
        dfk = [mm(d, fq[0, h, rows], TN) for d, (j, h, rows) in zip(dp, half)]
        dfq = [mm(d, fk[0, h, rows]) for d, (j, h, rows) in zip(dp, half)]
        for i, (j, h, rows) in enumerate(half):
            dfq_o[0, h, rows] = dfq[i] + inter[i]
            dfk_o[0, h, rows] = dfk[i]
            dva_o[0, h, rows] = dva[i]


def close_kernel(
    b, pos, units, attend, fq, fk, fqt, fkt, va, dfq, dfk, dva, ccol, ucol, pack, l1, st, wmix, gv, back,
    m00_o, m01_o, m10_o, m11_o, gnk_o, gns_o,
    acc_s, gm_s, gate_s, vsum_s, big_s,
    *, seqs_total,
):
    seqs = seqs_total
    chunk = units.shape[1] // 2
    nz = m00_o.shape[0]
    lane = lanes_of((chunk, 128))
    row, col = lower_tri(chunk)
    upper = jnp.where(row <= col, 1.0, 0.0).astype(BF16)
    zcols = pack[pack.shape[0] - 1].astype(F32)
    arrived = unpack_states(pack, b, zcols, last=64)
    wide = lanes_of((128, 128))

    @pl.when(b == 0)
    def _():
        gate_s[...] = jnp.zeros_like(gate_s)
        vsum_s[...] = jnp.zeros_like(vsum_s)

    pairs = pairs_of(chunk)
    spans = [slice(j * chunk, (j + 1) * chunk) for j in range(2)]
    cums = [ccol[0, rows] for rows in spans]
    freshs = [ucol[0, rows] for rows in spans]
    douts = [jnp.exp(cum[chunk - 1 : chunk] - cum) * fresh for cum, fresh in zip(cums, freshs)]
    nears = []
    for j, h, rows in pairs:
        adj = arrived[h]
        if j == 0:
            adj = l1[0, h] + jnp.exp(ccol[0, 2 * chunk - 1 : 2 * chunk, h : h + 1]) * adj
        zs = adj[:, 64:65] + adj[:, 65:66]
        high = low(zs).astype(F32)
        nears.append(low(jnp.where(wide == 64, high, jnp.where(wide == 65, zs - high, adj))))
    dk_fars = [mm(va[0, h, rows], near, NT) for near, (j, h, rows) in zip(nears, pairs)]
    dv_fars = [mm(fk[0, h, rows], near) for near, (j, h, rows) in zip(nears, pairs)]
    kds, qds, levels = [], [], []
    pqs, pks, dvs = [], [], []
    for i, (j, h, rows) in enumerate(pairs):
        d = douts[j][:, h : h + 1]
        keys, queries = fk[0, h, rows].astype(F32), fq[0, h, rows].astype(F32)
        dk_far = d * dk_fars[i]
        dk = dk_far + dfk[0, h, rows]
        dq = dfq[0, h, rows]
        kds.append(jnp.sum(keys * dk, axis=1, keepdims=True))
        qds.append(jnp.sum(queries * dq, axis=1, keepdims=True))
        passed = st[0, h, j].astype(F32) * nears[i].astype(F32)
        passed = jnp.sum(jnp.sum(passed, axis=0, keepdims=True), axis=1, keepdims=True)
        total = jnp.sum(jnp.sum(keys * dk_far, axis=0, keepdims=True), axis=1, keepdims=True)
        levels.append(total + jnp.exp(cums[j][chunk - 1 : chunk, h : h + 1]) * passed)
        dvs.append(dva[0, h, rows] + d * dv_fars[i])
        pks.append(low(dk * fkt[0, h, rows].astype(F32)))
        pqs.append(low(dq * fqt[0, h, rows].astype(F32)))
    grads = [
        [mm(jnp.concatenate(ps[4 * j + 2 * p : 4 * j + 2 * p + 2], axis=1), back[p]) for ps in (pqs, pks) for p in range(2)]
        for j in range(2)
    ]
    bias_sum = jnp.zeros((1, 128), F32)
    gms = []
    for j in range(2):
        kd = qd = jnp.zeros((chunk, 128), F32)
        level = jnp.zeros((1, 128), F32)
        for h in range(4):
            kd = jnp.where(lane == h, kds[4 * j + h], kd)
            qd = jnp.where(lane == h, qds[4 * j + h], qd)
            level = jnp.where(lanes_of((1, 128)) == h, levels[4 * j + h], level)
        dlog = tri_sum(upper, qd - kd) + level
        dlogit = jnp.where(lane < 4, freshs[j] * dlog - (1.0 - freshs[j]) * kd, 0.0)
        bias_sum += jnp.sum(dlogit, axis=0, keepdims=True)
        values = [jnp.where(lane < 64, dvs[4 * j + 2 * p], swap_halves(dvs[4 * j + 2 * p + 1])) for p in range(2)]
        gm = jnp.concatenate([low(x) for x in (*grads[j], *values, dlogit)], axis=1)
        gm_s[pl.ds(pl.multiple_of((2 * b + j) * chunk, chunk), chunk), :] = gm
        gms.append(gm)
    normed = [mm(gm, wmix[...], NT) for gm in gms]
    vsum_s[0:1] += sum(jnp.sum(n * units[0, rows], axis=0, keepdims=True) for n, rows in zip(normed, spans))
    vsum_s[1:2] += sum(jnp.sum(n, axis=0, keepdims=True) for n in normed)
    first = pos[3] == 0
    gnk_o[0] = jnp.where(first, normed[0], normed[1])
    gns_o[0] = low(jnp.where(first, normed[1], normed[0]))
    gate_s[0:1] += bias_sum

    @pl.when(b == seqs - 1)
    def _():
        width = acc_s.shape[0]
        acc_s[...] = mm(attend[...].reshape(gm_s.shape[0], width), gm_s[...], TN)
        table = jnp.concatenate(
            [jnp.zeros((4, width), F32), vsum_s[0:2], gv[0:2], jnp.zeros((120, width), F32)], axis=0
        ).T
        total = gate_s[0:1]
        high = low(total).astype(F32)
        rest = jnp.broadcast_to(total - high, (8, 128))
        both = pltpu.roll(jnp.broadcast_to(high, (8, 128)), 8, 1) + pltpu.roll(rest, 12, 1)
        biases = jnp.broadcast_to(both[0:1], (width, 128))
        side = jnp.where(lanes_of((width, 128)) < 4, acc_s[:, 768:896], table) + biases
        big_s[:, 0:768] = acc_s[:, 0:768].astype(BF16)
        big_s[:, 768:896] = side.astype(BF16)
        for my in range(2):
            for mx in range(2):
                for mz in range(nz):
                    at = pl.multiple_of(chip_row(pos, mz, mx, my), 32)
                    (m00_o, m01_o, m10_o, m11_o)[2 * my + mx][mz] = big_s[pl.ds(at, 32), :]


def final_kernel(pos, keep, recv, mix_o, gate_o, bias_o, *vec_o):
    first = pos[3] == 0
    mine, theirs = keep[...], recv[...]
    halves = (jnp.where(first, mine, theirs), jnp.where(first, theirs, mine))
    width = mix_o.shape[1] // 6
    for i in range(3):
        for s in range(2):
            mix_o[:, (2 * i + s) * width : (2 * i + s + 1) * width] = halves[s][:, i * width : (i + 1) * width]
    sides = [half[:, 3 * width :] for half in halves]
    lane = lanes_of(sides[0].shape)
    both = jnp.concatenate([sides[0] + sides[1], sides[0], sides[1], jnp.zeros((80, 128), F32)], axis=0).T
    gate_o[0:4] = both[0:4, 16:32]
    gate_o[4:8] = both[0:4, 32:48]
    for i, out in enumerate(vec_o):
        out[...] = both[4 + i, 0:16]
    sums = [side[0:8] + pltpu.roll(side[0:8], 124, 1) for side in sides]
    row = jnp.where(lane[0:8] < 4, pltpu.roll(sums[0], 120, 1), pltpu.roll(sums[1], 124, 1))
    bias_o[...] = row[0, 0:8]


def input_kernel(b, x, gm, keep, recv, vec, o, done_o):
    done_o[...] = jnp.zeros_like(done_o)
    unit, inv = norm_of(x[0].astype(F32))
    grad = keep[0] + recv[0].astype(F32)
    o[0] = gm[0] + norm_back(grad * vec[4:5], unit, inv)


def hold_kernel(*refs):
    sems = refs[-1]
    count = (len(refs) - 1) // 2
    copies = [
        pltpu.make_async_copy(refs[i], refs[count + i], sems.at[i]) for i in range(count)
    ]
    for copy in copies:
        copy.start()
    for copy in copies:
        copy.wait()


def halves_kernel(by_x, by_y, x_half, y_half, sems):
    half = x_half.shape[0]
    copies = [
        pltpu.make_async_copy(by_x.at[pl.ds(0, half)], x_half, sems.at[0]),
        pltpu.make_async_copy(by_y.at[pl.ds(half, half)], y_half, sems.at[1]),
    ]
    for copy in copies:
        copy.start()
    for copy in copies:
        copy.wait()


def gather_kernel(*refs):
    parts, out, sems = refs[:-2], refs[-2], refs[-1]
    copies, at = [], 0
    for i, part in enumerate(parts):
        copies.append(pltpu.make_async_copy(part, out.at[pl.ds(at, part.shape[0])], sems.at[i]))
        at += part.shape[0]
    for copy in copies:
        copy.start()
    for copy in copies:
        copy.wait()


def pause_kernel(out):
    out[...] = jnp.zeros_like(out)


def join_kernel(pos, *refs, axis):
    parts, out, sems = refs[:-2], refs[-2], refs[-1]
    copies = [
        pltpu.make_async_copy(part, out.at[pos[axis] ^ i], sems.at[i]) for i, part in enumerate(parts)
    ]
    for copy in copies:
        copy.start()
    for copy in copies:
        copy.wait()


def pair_sum_kernel(keep, recv, okeep, orecv, x_keep, x_send, y_keep, y_send):
    half = x_keep.shape[1]
    rows = keep.shape[3]
    first, second = slice(0, half), slice(half, 2 * half)
    for i in range(2):
        for my, mx, zs, out in ((i, 0, first, x_keep), (i, 1, first, x_send), (0, i, second, y_keep), (1, i, second, y_send)):
            out[i, :, 0:rows] = low(keep[my, mx, zs].astype(F32) + recv[my, mx, zs].astype(F32))
            out[i, :, rows:] = low(okeep[my, mx, zs].astype(F32) + orecv[my, mx, zs].astype(F32))


def half_sum_kernel(x_keep, x_recv, y_keep, y_recv, x_own, x_far, y_own, y_far):
    for keep, recv, own, far in ((x_keep, x_recv, x_own, x_far), (y_keep, y_recv, y_own, y_far)):
        for i, out in ((0, own), (1, far)):
            out[...] = low(keep[i].astype(F32) + recv[i].astype(F32))


def line_sum_kernel(x_own, x_recv, y_own, y_recv, *outs):
    half = x_own.shape[0]
    for i in range(half):
        outs[i][...] = low(x_own[i].astype(F32) + x_recv[i].astype(F32))
        outs[half + i][...] = low(y_own[i].astype(F32) + y_recv[i].astype(F32))


def sum_of_four(refs):
    a, b, c, d = (ref[...].astype(F32) for ref in refs)
    return (a + b) + (c + d)


def mix_sum_kernel(m0, m1, m2, m3, *outs):
    total = sum_of_four((m0, m1, m2, m3))
    side = total[..., 768:896]
    rest = side - low(side).astype(F32)
    lane = lanes_of(side.shape)
    moved = jnp.where((lane >= 12) & (lane < 16), side + pltpu.roll(rest, 4, side.ndim - 1), side)
    for i, out in enumerate(outs):
        out[:, 0:768] = low(total[i, :, 0:768])
        out[:, 768:896] = low(moved[i])


def feed_last_kernel(a, b, c, d, up_o, down_o, out_o, done_o):
    done_o[...] = jnp.zeros_like(done_o)
    total = sum_of_four((a, b, c, d))
    rows = up_o.shape[0]
    up_o[...] = total[0:rows]
    down_o[...] = total[rows : 2 * rows]
    out_o[...] = total[2 * rows :]


def mix_last_kernel(pos, a, b, c, d, keep_o, send_o):
    total = sum_of_four((a, b, c, d))
    rows = keep_o.shape[0]
    first = pos[3] == 0
    keep_o[...] = jnp.where(first, total[:rows], total[rows:])
    send_o[...] = jnp.where(first, total[rows:], total[:rows])


def call(kernel, steps, ins, outs, scratch=(), us=1.0, name=None, limit=12, unroll=False):
    def spec(kind):
        if kind in "da":
            return pl.BlockSpec(memory_space=pl.ANY)
        return pl.BlockSpec(memory_space=pltpu.SMEM if kind == "m" else pltpu.VMEM)

    kinds = [kind for kind, _ in ins]
    out_kinds = [kind for kind, _, _ in outs]
    all_kinds = kinds + out_kinds + ["w"] * len(scratch)

    def run(*refs):
        used = [(kind, ref) for kind, ref in zip(all_kinds, refs) if kind != "d"]
        if not steps:
            kernel(*[ref for _, ref in used])
            return

        def one(b, carry):
            kernel(b, *[ref.at[pl.ds(b, 1)] if kind == "s" else ref for kind, ref in used])
            return carry

        lax.fori_loop(0, steps, one, 0, unroll=unroll)

    return pl.pallas_call(
        run,
        in_specs=[spec(kind) for kind in kinds],
        out_specs=[spec(kind) for kind in out_kinds],
        out_shape=[jax.ShapeDtypeStruct(shape, dtype) for _, shape, dtype in outs],
        scratch_shapes=list(scratch),
        compiler_params=pltpu.CompilerParams(vmem_limit_bytes=limit * 1024 * 1024),
        cost_estimate=pl.CostEstimate(flops=int(us * 1.15e9), bytes_accessed=0, transcendentals=0),
        name=name,
    )(*[a for _, a in ins])


def xor_with(a, mask, count):
    return lax.ppermute(a, BOTH, [(i, i ^ mask) for i in range(count)])


def body(
    inputs, cotangent, mix_weight, gate_weight, gate_bias, out_weight, gain_first, shift_first, gain_second,
    shift_second, up_weight, down_weight, random_maps,
):
    dp, tensor = lax.axis_size("dp"), lax.axis_size("tensor")
    count = dp * tensor
    place_dp, place_t = lax.axis_index("dp"), lax.axis_index("tensor")
    seqs, chunk, width = inputs.shape
    heads, head = random_maps.shape[0], random_maps.shape[1]
    hidden = up_weight.shape[1]
    core = place_t % 2
    first = core == 0
    direct = dp == 8
    nz = 4
    if direct:
        pos = jnp.stack([place_dp // 2, place_dp % 2, place_t // 2, core]).astype(jnp.int32)
    else:
        pos = jnp.stack([jnp.zeros_like(core)] * 3 + [core]).astype(jnp.int32)
    swap_core = functools.partial(xor_with, mask=1, count=count)

    def mix_pack(mix_w, gate_w, vecs):
        rows = mix_w.shape[0]
        split = mix_w.reshape(rows, 3, 2, width // 2)
        sides = [v[:, None] for v in vecs]
        pad = jnp.zeros((rows, 120), BF16)
        return [
            jnp.concatenate(
                [split[:, 0, s], split[:, 1, s], split[:, 2, s], gate_w[:, 4 * s : 4 * s + 4]] + sides + [pad], axis=1
            )
            for s in range(2)
        ]

    def join(parts, axis, after=()):
        (out,) = call(
            functools.partial(join_kernel, axis=axis), 0, [("m", pos)] + [("a", a) for a in parts] + [("d", a) for a in after],
            [("w", (len(parts), *parts[0].shape), parts[0].dtype)],
            scratch=[pltpu.SemaphoreType.DMA((len(parts),))], name="join",
        )
        return out

    def pause(after, us):
        (out,) = call(
            pause_kernel, 0, [("d", a) for a in after], [("w", (8, 128), F32)], us=us, name="pause",
        )
        return out

    def from_plane(pieces):
        return [pieces[0], xor_with(pieces[1], 4, count), xor_with(pieces[2], 2, count), xor_with(pieces[3], 6, count)]

    other_in = swap_core(inputs)
    vectors = (gain_first, shift_first, gain_second, shift_second)
    long = 2 * chunk
    unit, cot_t = call(
        prepare_kernel, seqs, [("m", pos), ("s", inputs), ("s", other_in), ("s", cotangent)],
        [("s", (seqs, long, width), F32), ("s", (seqs, width, chunk), BF16)], us=2.5, name="prepare",
    )
    if direct:
        rows = mix_weight.shape[0]
        columns = jnp.pad(gate_weight.T, ((0, 16 - heads), (0, 0)))
        place = lax.broadcasted_iota(jnp.int32, columns.shape, 0)
        for i, v in enumerate(vectors):
            columns = jnp.where(place == heads + i, lax.broadcast_in_dim(v, columns.shape, (1,)), columns)
        keep, send = call(
            pack_kernel, 0, [("m", pos), ("w", mix_weight), ("w", columns)], [("w", (rows, 896), BF16)] * 2, name="pack",
        )
        pair = join([keep, swap_core(send)], 3)
        line = join([pair] + [xor_with(pair, 8 * m, count) for m in range(1, nz)], 0, after=[unit])
        w_pieces = [line] + [xor_with(line, m, count) for m in (4, 2, 6)]
        block = jnp.concatenate([up_weight, down_weight.T, out_weight], axis=0)
        (block,) = call(
            hold_kernel, 0, [("a", block), ("d", unit)],
            [("w", block.shape, BF16)], scratch=[pltpu.SemaphoreType.DMA((1,))], name="hold",
        )
        ff_line = join([block] + [xor_with(block, 8 * m, count) for m in range(1, nz)], 0, after=[line])
        by_x, by_y = xor_with(ff_line, 4, count), xor_with(ff_line, 2, count)
    else:
        whole = [
            lax.all_gather(a, BOTH, axis=0, tiled=True) for a in (mix_weight, gate_weight, out_weight) + vectors
        ]
        p0, p1 = mix_pack(whole[0], whole[1], whole[3:])
        blocks = jnp.where(first, p0, p1).reshape(nz, 2, 2, 2, 16, 896)
        w_pieces = [blocks[:, mx, my] for my, mx in ((0, 0), (0, 1), (1, 0), (1, 1))]
        up_all = lax.all_gather(up_weight, BOTH, axis=0, tiled=False).reshape(dp, tensor, -1, hidden)
        dn_all = lax.all_gather(down_weight.T, BOTH, axis=0, tiled=False).reshape(dp, tensor, -1, hidden)
        up_all = jnp.moveaxis(up_all, 1, 0).reshape(2, 2, nz, 2, -1, hidden)
        dn_all = jnp.moveaxis(dn_all, 1, 0).reshape(2, 2, nz, 2, -1, hidden)
        out_all = whole[2].reshape(nz, 2, 2, 2, 16, width).transpose(2, 3, 0, 1, 4, 5)
        ff_all = jnp.concatenate([up_all, dn_all, out_all], axis=4)
        ff_all = jnp.where(first, ff_all, ff_all[:, ::-1])
        ff_own, ff_other = (
            jnp.concatenate([ff_all[my, mc, :, mx] for my in range(2) for mx in range(2)]) for mc in range(2)
        )

    maps = lax.dynamic_slice_in_dim(random_maps, core * 4, 4, 0)
    zero = jnp.zeros((head, head), BF16)
    maps_pair = jnp.stack(
        [
            jnp.concatenate(
                [jnp.concatenate([maps[2 * p], zero], 1), jnp.concatenate([zero, maps[2 * p + 1]], 1)], 0
            )
            for p in range(2)
        ]
    )
    flip = jnp.swapaxes(maps, 1, 2)
    maps_back = jnp.stack(
        [
            jnp.concatenate(
                [
                    jnp.concatenate([flip[2 * p], zero], 1),
                    jnp.concatenate([-flip[2 * p], zero], 1),
                    jnp.concatenate([zero, flip[2 * p + 1]], 1),
                    jnp.concatenate([zero, -flip[2 * p + 1]], 1),
                ],
                0,
            )
            for p in range(2)
        ]
    )
    bias = jnp.pad(lax.dynamic_slice_in_dim(gate_bias, core * 4, 4, 0), (0, 124))[None]

    tokens = seqs * long
    feats = (seqs, 4, long, 128)
    npack = 2 * seqs + 1
    attend, fk, fkl, fkt, va, ccol, ucol, crow, smid, pack, wmix, vec, vbar = call(
        project_kernel, seqs,
        [("m", pos), ("s", unit)] + [("a", w) for w in w_pieces] + [("w", bias), ("w", maps_pair)],
        [
            ("s", (seqs, long, width), BF16), ("s", feats, BF16), ("s", feats, BF16), ("s", feats, BF16), ("s", feats, BF16),
            ("s", (seqs, long, 128), F32), ("s", (seqs, long, 128), F32),
            ("s", (seqs, 2, 8, chunk), F32),
            ("s", (seqs, 4, 128, 128), F32),
            ("w", (npack, 128, 128), BF16), ("w", (width, 896), BF16), ("w", (8, width), F32),
            ("w", (8, width // 2), F32),
        ],
        scratch=[pltpu.VMEM((nz, 2, 2, 2, 16, 896), BF16), pltpu.SemaphoreType.DMA((4,))], us=12, name="project",
    )
    ahead = [(i, i + 2) for i in range(count) if (i % tensor) < 2]
    arrived = lax.ppermute(pack, BOTH, ahead)
    fq, fql, fqt = call(
        query_kernel, seqs, [("s", attend), ("w", wmix), ("w", maps_pair)], [("s", feats, BF16)] * 3, us=0.3, name="query",
    )
    (o_loc,) = call(
        local_kernel, seqs,
        [("s", fq), ("s", fk), ("s", fql), ("s", fkl), ("s", va), ("s", ccol), ("s", crow)],
        [("s", feats, F32)], us=0.3, name="local",
    )
    if direct:
        half_z = nz // 2
        far_shape = (half_z, *ff_line.shape[1:])
        x_half, y_half = call(
            halves_kernel, 0, [("a", by_x), ("a", by_y), ("d", arrived), ("d", o_loc)], [("w", far_shape, BF16)] * 2,
            scratch=[pltpu.SemaphoreType.DMA((2,))], us=0.3, name="halves",
        )
        near_parts = [ff_line, by_x, by_y]
        (ff_near,) = call(
            gather_kernel, 0, [("a", a) for a in near_parts] + [("d", x_half)],
            [("w", (3 * nz, *ff_line.shape[1:]), BF16)], scratch=[pltpu.SemaphoreType.DMA((3,))], us=0.5, name="near",
        )
        before_finish = [x_half]
    else:
        before_finish = []
    (inv_root, turn, st, att_keep, att_send) = call(
        finish_kernel, seqs,
        [("m", pos), ("s", o_loc), ("s", fq), ("s", ccol), ("w", arrived), ("s", smid), ("w", vbar)]
        + [("d", a) for a in before_finish],
        [
            ("s", feats, F32), ("s", feats, F32), ("s", (seqs, 4, 2, 128, 128), BF16),
            ("s", (seqs, chunk, width // 2), BF16), ("s", (seqs, chunk, width // 2), BF16),
        ],
        us=0.3, name="finish",
    )
    att_recv = swap_core(att_send)
    if direct:
        near_other = swap_core(ff_near)
        far_parts = [xor_with(x_half, 2, count), xor_with(y_half, 4, count)]
        (ff_far,) = call(
            gather_kernel, 0, [("a", a) for a in far_parts] + [("d", att_keep)],
            [("w", ff_line.shape, BF16)], scratch=[pltpu.SemaphoreType.DMA((2,))], name="gather",
        )
        far_other = swap_core(ff_far)
    else:
        ff_near, ff_far, near_other, far_other = ff_own[: 3 * nz], ff_own[3 * nz :], ff_other[: 3 * nz], ff_other[3 * nz :]

    own = seqs * chunk
    nrows = ff_near.shape[1]
    payload, out_payload = (2, 2, nz, nrows - 16, hidden), (2, 2, nz, 16, hidden)
    rows_low, rows_full = ("w", (own, width), BF16), ("w", (own, width), F32)
    work = [
        pltpu.VMEM((width, 2 * hidden), BF16), pltpu.VMEM((width, 2 * hidden), BF16),
        pltpu.VMEM((own, 2 * hidden), BF16), pltpu.VMEM((own, 2 * hidden), BF16),
    ]
    big = pltpu.VMEM((width, 2 * hidden), BF16)
    g_send, *fed = call(
        feed_first_kernel, 0,
        [("m", pos)] + [
            ("w", a) for a in (
                att_keep, att_recv, inputs, cotangent, cot_t, vec, ff_near, ff_far, near_other, far_other
            )
        ],
        [
            ("w", payload, BF16), rows_full, rows_full, rows_full, rows_low, ("w", (width, own), BF16), rows_low,
            ("w", (width, width), BF16),
        ],
        scratch=[*work, big], us=10, name="feed_first", limit=18,
    )
    g_recv = swap_core(g_send)
    output, grad_middle, ga_keep, ga_send, g_keep, o_keep, o_send, grad_vec = call(
        feed_second_kernel, 0,
        [("m", pos)] + [("w", a) for a in (cotangent, cot_t, vec, ff_near, ff_far, *fed)],
        [
            ("w", (seqs, chunk, width), BF16), ("w", (seqs, chunk, width), F32),
            ("w", (seqs, chunk, width // 2), BF16), ("w", (seqs, chunk, width // 2), BF16),
            ("w", payload, BF16), ("w", out_payload, BF16), ("w", out_payload, BF16), ("w", (8, width), F32),
        ],
        scratch=[
            *work, pltpu.VMEM((own, width), BF16), big,
        ],
        us=10, name="feed_second", limit=18,
    )
    ga_recv = swap_core(ga_send)

    if direct:
        o_recv = swap_core(o_send)
        half_z = nz // 2
        two, one = (2, half_z, nrows, hidden), (half_z, nrows, hidden)
        x_keep, x_send, y_keep, y_send = call(
            pair_sum_kernel, 0, [("w", g_keep), ("w", g_recv), ("w", o_keep), ("w", o_recv)], [("w", two, BF16)] * 4,
            us=0.6, name="pair_sum",
        )
        x_recv, y_recv = xor_with(x_send, 4, count), xor_with(y_send, 2, count)
        before_adjoint = [x_keep]
    else:
        before_adjoint = []
        g_keep, g_send = (jnp.concatenate(parts, axis=3) for parts in ((g_keep, o_keep), (g_send, o_send)))
        by_core = jnp.where(first, jnp.stack([g_keep, g_send]), jnp.stack([g_send, g_keep]))
        by_rows = by_core.transpose(3, 2, 1, 0, 4, 5)
        rows_up = (nrows - 16) // 2
        ups = by_rows[..., :rows_up, :].reshape(nz * 2, 4, rows_up, hidden).transpose(1, 0, 2, 3)
        dns = by_rows[..., rows_up : 2 * rows_up, :].reshape(nz * 2, 4, rows_up, hidden).transpose(1, 0, 2, 3)
        ups = ups.reshape(4, dp, -1, hidden).transpose(1, 0, 2, 3)
        dns = dns.reshape(4, dp, -1, hidden).transpose(1, 0, 2, 3)
        outs = by_rows[..., 2 * rows_up :, :].reshape(width, width)

        def reduced(a):
            return lax.psum_scatter(a.astype(F32).reshape(count, -1, a.shape[-1]), BOTH, scatter_dimension=0)

        up_grad, down_grad, out_grad = reduced(ups), reduced(dns).T, reduced(outs)

    g, scaled, l1, pack_b = call(
        adjoint_kernel, seqs,
        [("m", pos), ("s", ga_keep), ("s", ga_recv), ("s", inv_root), ("s", turn), ("s", fq), ("s", ccol)]
        + [("d", a) for a in before_adjoint],
        [
            ("s", feats, BF16), ("s", feats, BF16), ("s", (seqs, 4, 128, 128), F32), ("w", (npack, 128, 128), BF16),
        ],
        us=0.3, name="adjoint",
    )
    behind = [(i, i - 2) for i in range(count) if (i % tensor) >= 2]
    arrived_b = lax.ppermute(pack_b, BOTH, behind)
    dfq, dfk, dva = call(
        local_back_kernel, seqs,
        [("s", fq), ("s", fk), ("s", va), ("s", g), ("s", scaled), ("s", st), ("s", ccol), ("s", crow)],
        [("s", feats, F32), ("s", feats, F32), ("s", feats, F32)],
        us=0.3, name="local_back",
    )
    before_close = []
    if direct:
        x_own, x_far, y_own, y_far = call(
            half_sum_kernel, 0, [("w", a) for a in (x_keep, x_recv, y_keep, y_recv)] + [("d", dfq)],
            [("w", one, BF16)] * 4, us=0.4, name="half_sum",
        )
        x_recv, y_recv = xor_with(x_far, 2, count), xor_with(y_far, 4, count)
        before_close = [x_own]
    *m_pieces, gn_keep, gn_send = call(
        functools.partial(close_kernel, seqs_total=seqs), seqs,
        [("m", pos), ("s", unit), ("w", attend), ("s", fq), ("s", fk), ("s", fqt), ("s", fkt), ("s", va), ("s", dfq),
         ("s", dfk), ("s", dva), ("s", ccol), ("s", ucol), ("w", arrived_b), ("s", l1), ("s", st),
         ("w", wmix), ("w", grad_vec), ("w", maps_back)] + [("d", a) for a in before_close],
        [*[("w", (nz, 32, 896), BF16)] * 4, ("s", (seqs, chunk, width), F32), ("s", (seqs, chunk, width), BF16)],
        scratch=[
            pltpu.VMEM((width, 896), F32), pltpu.VMEM((tokens, 896), BF16), pltpu.VMEM((8, 128), F32),
            pltpu.VMEM((8, width), F32), pltpu.VMEM((width, 896), BF16),
        ],
        us=14.7, name="close", unroll=False,
    )
    if direct:
        g_line = call(
            line_sum_kernel, 0, [("w", a) for a in (x_own, x_recv, y_own, y_recv)] + [("d", gn_keep)],
            [("w", (nrows, hidden), BF16)] * nz, us=0.4, name="line_sum",
        )
        m_parts = from_plane(m_pieces)
    gn_recv = swap_core(gn_send)
    def finish_input(after):
        return call(
            input_kernel, seqs,
            [("s", inputs), ("s", grad_middle), ("s", gn_keep), ("s", gn_recv), ("w", vec)] + [("d", a) for a in after],
            [("s", (seqs, chunk, width), F32), ("w", (8, 128), F32)], us=0.3, name="input_grad",
        )

    if direct:
        m_plane = call(
            mix_sum_kernel, 0, [("w", a) for a in m_parts] + [("d", pause([g_line[0]], 40)), ("d", gn_recv)],
            [("w", (32, 896), BF16)] * nz, us=0.4, name="mix_sum",
        )
        input_grad, input_done = finish_input([m_plane[0]])
        g_parts = [g_line[0]] + [xor_with(g_line[m], 8 * m, count) for m in range(1, nz)]
        up_grad, down_back, out_grad, feed_done = call(
            feed_last_kernel, 0, [("w", a) for a in g_parts],
            [("w", shape, F32) for shape in (up_weight.shape, down_weight.shape[::-1], out_weight.shape, (8, 128))],
            us=0.3, name="feed_last",
        )
        down_grad = down_back.T
        mix_parts = [m_plane[0]] + [xor_with(m_plane[m], 8 * m, count) for m in range(1, nz)]
        m_keep, m_send = call(
            mix_last_kernel, 0, [("m", pos)] + [("w", a) for a in mix_parts] + [("d", feed_done), ("d", input_done)],
            [("w", (mix_weight.shape[0], 896), F32)] * 2, name="mix_last",
        )
        m_recv = swap_core(m_send)
    else:
        input_grad, input_done = finish_input([])
        m_all = jnp.stack(m_pieces).astype(F32).reshape(2, 2, nz, 32, 896)
        mine_rows = m_all.transpose(2, 1, 0, 3, 4).reshape(count, -1, 896)
        keep_part = lax.psum_scatter(mine_rows * jnp.where(first, 1.0, 0.0), BOTH, scatter_dimension=0)
        far_part = lax.psum_scatter(mine_rows * jnp.where(first, 0.0, 1.0), BOTH, scatter_dimension=0)
        m_keep = jnp.where(first, keep_part, far_part)
        m_recv = jnp.where(first, far_part, keep_part)
    if direct:
        mix_grad, gate_back, bias_grad, *per_row = call(
            final_kernel, 0, [("m", pos), ("w", m_keep), ("w", m_recv)],
            [("w", mix_weight.shape, F32), ("w", gate_weight.shape[::-1], F32), ("w", (heads,), F32)]
            + [("w", gain_first.shape, F32)] * 4,
            us=1.2, name="final",
        )
        gate_grad = gate_back.T
    else:
        m_low = jnp.where(first, m_keep, m_recv)
        m_high = jnp.where(first, m_recv, m_keep)
        mix_grad = jnp.concatenate(
            [part[:, 256 * i : 256 * i + 256] for i in range(3) for part in (m_low, m_high)], axis=1
        )
        gate_grad = jnp.concatenate([m_low[:, 768:772], m_high[:, 768:772]], axis=1)
        bias_grad = jnp.concatenate([m[0, 776:780] + m[0, 780:784] for m in (m_low, m_high)])
        per_row = [m_keep[:, 772 + i] + m_recv[:, 772 + i] for i in range(4)]
    return (
        output, input_grad, mix_grad, gate_grad, bias_grad, out_grad,
        *per_row, up_grad, down_grad,
    )


def solution(mesh):
    rows, spread = P(("dp", "tensor"), None), P(("dp", "tensor"))
    tokens = P("dp", "tensor", None)
    in_specs = (
        tokens, tokens, rows, rows, P(), rows, spread, spread, spread, spread, P("dp", "tensor"), P("tensor", "dp"), P(),
    )
    out_specs = (
        tokens, tokens, rows, rows, P(), rows, spread, spread, spread, spread, P("dp", "tensor"), P("tensor", "dp"),
    )
    return jax.shard_map(body, mesh=mesh, in_specs=in_specs, out_specs=out_specs, check_vma=False)
```

profile of v0, /device:TPU:0, one launch (start us, length us, event | category | flops | bytes accessed | tf_op | source)
XLA Modules:
  0.0 148.3 jit_solution(16193015235224201177)
XLA Ops:
  5.5 2.8 %collective-permute-start.2 = (bf16[2,16,896]{2,1,0:T(8,128)(2,1)S(1)}, bf16[2,16,896]{2,1,0:T(8,128)(2,1)S(1)}, u32[]{:S(2)}, u32[]{:S(2)}) collective-permute-start(bf16[2,16,896]{2,1,0:T(8,128)(2,1)S(1)} %join.3.refs_1_), channel_id=1, source_target_pairs={{0,8},{1,9},{2,10},{3,11},{4,12},{5,13},{6,14},{7,15},{8,0},{9,1},... | collective-permute-start | bytes 172040 | tf_op jit(solution)/shard_map/ppermute | solution.py:759
  8.3 2.6 %collective-permute-start.3 = (bf16[2,16,896]{2,1,0:T(8,128)(2,1)S(1)}, bf16[2,16,896]{2,1,0:T(8,128)(2,1)S(1)}, u32[]{:S(2)}, u32[]{:S(2)}) collective-permute-start(bf16[2,16,896]{2,1,0:T(8,128)(2,1)S(1)} %join.3.refs_1_), channel_id=1, source_target_pairs={{0,16},{1,17},{2,18},{3,19},{4,20},{5,21},{6,22},{7,23},{8,24},{9,... | collective-permute-start | bytes 172040 | tf_op jit(solution)/shard_map/ppermute | solution.py:759
  10.9 1.9 %prepare.1 = (f32[3,512,512]{2,1,0:T(8,128)S(1)}, bf16[3,512,256]{2,1,0:T(8,128)(2,1)S(1)}) custom-call(s32[4]{0:T(128)S(1)} %pad_add_fusion.refs_0_, bf16[3,256,512]{2,1,0:T(8,128)(2,1)S(1)} %copy-done.2, bf16[3,256,512]{2,1,0:T(8,128)(2,1)S(1)} %collective-permute-done.refs_2_, bf16[3,256,512]{2,1,0:T(8,128)(2,1)S(1)} %copy-done.3), custom_call_target="tpu_custom_call" | custom-call | flops 2875000064 | tf_op jit(solution)/shard_map/prepare/pallas_call | solution.py:746
  13.7 3.8 %collective-permute-start.10 = (bf16[144,512]{1,0:T(8,128)(2,1)S(1)}, bf16[144,512]{1,0:T(8,128)(2,1)S(1)}, u32[]{:S(2)}, u32[]{:S(2)}) collective-permute-start(bf16[144,512]{1,0:T(8,128)(2,1)S(1)} %hold.1.refs_1_), channel_id=1, source_target_pairs={{0,24},{1,25},{2,26},{3,27},{4,28},{5,29},{6,30},{7,31},{8,16},{9,... | collective-permute-start | bytes 442376 | tf_op jit(solution)/shard_map/ppermute | solution.py:759
  22.1 2.5 %collective-permute-start.9 = (bf16[144,512]{1,0:T(8,128)(2,1)S(1)}, bf16[144,512]{1,0:T(8,128)(2,1)S(1)}, u32[]{:S(2)}, u32[]{:S(2)}) collective-permute-start(bf16[144,512]{1,0:T(8,128)(2,1)S(1)} %hold.1.refs_1_), channel_id=1, source_target_pairs={{0,16},{1,17},{2,18},{3,19},{4,20},{5,21},{6,22},{7,23},{8,24},{9,... | collective-permute-start | bytes 442376 | tf_op jit(solution)/shard_map/ppermute | solution.py:759
  24.9 4.5 %collective-permute-done.8.refs_2_ = bf16[144,512]{1,0:T(8,128)(2,1)S(1)} collective-permute-done((bf16[144,512]{1,0:T(8,128)(2,1)S(1)}, bf16[144,512]{1,0:T(8,128)(2,1)S(1)}, u32[]{:S(2)}, u32[]{:S(2)}) %collective-permute-start.8) | collective-permute-done | bytes 147488 | tf_op jit(solution)/shard_map/ppermute | solution.py:759
  35.3 8.8 %project.1 = (bf16[3,512,512]{2,1,0:T(8,128)(2,1)S(1)}, bf16[3,4,512,128]{3,2,1,0:T(8,128)(2,1)S(1)}, bf16[3,4,512,128]{3,2,1,0:T(8,128)(2,1)S(1)}, bf16[3,4,512...) custom-call(s32[4]{0:T(128)S(1)} %pad_add_fusion.refs_0_, ...), custom_call_target="tpu_custom_call" | custom-call | flops 13799999488 | tf_op jit(solution)/shard_map/project/pallas_call | solution.py:746
  44.2 2.4 %collective-permute-start.13 = (bf16[7,128,128]{2,1,0:T(8,128)(2,1)S(1)}, bf16[7,128,128]{2,1,0:T(8,128)(2,1)S(1)}, u32[]{:S(2)}, u32[]{:S(2)}) collective-permute-start(bf16[7,128,128]{2,1,0:T(8,128)(2,1)S(1)} %get-tuple-element.104), channel_id=1, source_target_pairs={{0,2},{1,3},{4,6},{5,7},{8,10},{9,11},{12,14},{13,15},{16,18},{17,... | collective-permute-start | bytes 688136 | tf_op jit(solution)/shard_map/ppermute | solution.py:899
  46.6 3.6 %query.1 = (bf16[3,4,512,128]{3,2,1,0:T(8,128)(2,1)S(1)}, bf16[3,4,512,128]{3,2,1,0:T(8,128)(2,1)S(1)}, bf16[3,4,512,128]{3,2,1,0:T(8,128)(2,1)S(1)}) custom-call(bf16[3,512,512]{2,1,0:T(8,128)(2,1)S(1)} %get-tuple-element.105.refs_0_.refs_2_, bf16[512,896]{1,0:T(8,128)(2,1)S(1)} %get-tuple-element.106.refs_1_.refs_16_, ...), custom_call_target="tpu_custom_call" | custom-call | flops 345000000 | tf_op jit(solution)/shard_map/query/pallas_call | solution.py:746
  50.2 3.3 %local.1.refs_3_.refs_1_ = f32[3,4,512,128]{3,2,1,0:T(8,128)S(1)} custom-call(bf16[3,4,512,128]{3,2,1,0:T(8,128)(2,1)S(1)} %get-tuple-element.107.refs_0_.refs_2_.refs_5_.refs_3_, bf16[3,4,512,128]{3,2,1,0:T(8,128)(2,1)S(1)} %get-tuple-element.108.refs_1_.refs_4_, bf16[3,4,512,128]{3,2,1,0:T(8,128)(2,1)S(1)} %get-tuple-element.109.refs_2_, ...), custom_call_target="tpu_custom_call" | custom-call | flops 345000000 | tf_op jit(solution)/shard_map/local/pallas_call | solution.py:746
  54.9 4.1 %finish.1 = (f32[3,4,512,128]{3,2,1,0:T(8,128)S(1)}, f32[3,4,512,128]{3,2,1,0:T(8,128)S(1)}, bf16[3,4,2,128,128]{4,3,2,1,0:T(8,128)(2,1)S(1)}, bf16[3,256,256]{2,1,0:T(8,128)(2,1)S(1)}, bf16[3,256,256]{2,1,0:T(8,128)(2,1)S(1)}) custom-call(s32[4]{0:T(128)S(1)} %pad_add_fusion.refs_0_, f32[3,4,512,128]{3,2,1,0:T(8,128)S(1)} %local.1.refs_3_.refs_1_, ...), custom_call_target="tpu_custom_call" | custom-call | flops 345000000 | tf_op jit(solution)/shard_map/finish/pallas_call | solution.py:746
  59.0 4.6 %collective-permute-done.14.refs_0_ = bf16[2,144,512]{2,1,0:T(8,128)(2,1)S(1)} collective-permute-done((bf16[2,144,512]{2,1,0:T(8,128)(2,1)S(1)}, bf16[2,144,512]{2,1,0:T(8,128)(2,1)S(1)}, u32[]{:S(2)}, u32[]{:S(2)}) %collective-permute-start.14) | collective-permute-done | bytes 294944 | tf_op jit(solution)/shard_map/ppermute | solution.py:759
  64.5 2.1 %collective-permute-done.16.refs_2_ = bf16[3,256,256]{2,1,0:T(8,128)(2,1)S(1)} collective-permute-done((bf16[3,256,256]{2,1,0:T(8,128)(2,1)S(1)}, bf16[3,256,256]{2,1,0:T(8,128)(2,1)S(1)}, u32[]{:S(2)}, u32[]{:S(2)}) %collective-permute-start.16) | collective-permute-done | bytes 393248 | tf_op jit(solution)/shard_map/ppermute | solution.py:759
  66.6 7.9 %feed_first.1 = (bf16[2,2,4,128,512]{4,3,2,1,0:T(8,128)(2,1)S(1)}, f32[768,512]{1,0:T(8,128)S(1)}, f32[768,512]{1,0:T(8,128)S(1)}, f32[768,512]{1,0:T(8,128)S(1)...) custom-call(s32[4]{0:T(128)S(1)} %pad_add_fusion.refs_0_, ...), custom_call_target="tpu_custom_call" | custom-call | flops 11500000256 | tf_op jit(solution)/shard_map/feed_first/pallas_call | solution.py:746
  74.7 9.4 %feed_second.1 = (bf16[3,256,512]{2,1,0:T(8,128)(2,1)}, f32[3,256,512]{2,1,0:T(8,128)S(1)}, bf16[3,256,256]{2,1,0:T(8,128)(2,1)S(1)}, bf16[3,256,256]{2,1,0:T(8,...) custom-call(s32[4]{0:T(128)S(1)} %pad_add_fusion.refs_0_, ...), custom_call_target="tpu_custom_call" | custom-call | flops 11500000256 | tf_op jit(solution)/shard_map/feed_second/pallas_call | solution.py:746
  88.6 5.2 %adjoint.1 = (bf16[3,4,512,128]{3,2,1,0:T(8,128)(2,1)S(1)}, bf16[3,4,512,128]{3,2,1,0:T(8,128)(2,1)S(1)}, f32[3,4,128,128]{3,2,1,0:T(8,128)S(1)}, bf16[7,128,128]{2,1,0:T(8,128)(2,1)S(1)}) custom-call(s32[4]{0:T(128)S(1)} %pad_add_fusion.refs_0_, bf16[3,256,256]{2,1,0:T(8,128)(2,1)S(1)} %get-tuple-element.131.refs_1_, ...), custom_call_target="tpu_custom_call" | custom-call | flops 345000000 | tf_op jit(solution)/shard_map/adjoint/pallas_call | solution.py:746
  95.2 5.3 %local_back.1 = (f32[3,4,512,128]{3,2,1,0:T(8,128)S(1)}, f32[3,4,512,128]{3,2,1,0:T(8,128)S(1)}, f32[3,4,512,128]{3,2,1,0:T(8,128)S(1)}) custom-call(bf16[3,4,512,128]{3,2,1,0:T(8,128)(2,1)S(1)} %get-tuple-element.107.refs_0_.refs_2_.refs_5_.refs_3_, bf16[3,4,512,128]{3,2,1,0:T(8,128)(2,1)S(1)} %get-tuple-element.108.refs_1_.refs_4_, ...), custom_call_target="tpu_custom_call" | custom-call | flops 345000000 | tf_op jit(solution)/shard_map/local_back/pallas_call | solution.py:746
  105.7 2.2 %collective-permute-done.22.refs_13_ = bf16[7,128,128]{2,1,0:T(8,128)(2,1)S(1)} collective-permute-done((bf16[7,128,128]{2,1,0:T(8,128)(2,1)S(1)}, bf16[7,128,128]{2,1,0:T(8,128)(2,1)S(1)}, u32[]{:S(2)}, u32[]{:S(2)}) %collective-permute-start.22) | collective-permute-done | bytes 229408 | tf_op jit(solution)/shard_map/ppermute | solution.py:1020
  108.0 12.4 %close.1 = (bf16[4,32,896]{2,1,0:T(8,128)(2,1)S(1)}, bf16[4,32,896]{2,1,0:T(8,128)(2,1)S(1)}, bf16[4,32,896]{2,1,0:T(8,128)(2,1)S(1)}, bf16[4,32,896]{2,1,0:T(8,...) custom-call(s32[4]{0:T(128)S(1)} %pad_add_fusion.refs_0_, f32[3,512,512]{2,1,0:T(8,128)S(1)} %copy-done.7, ...), custom_call_target="tpu_custom_call" | custom-call | flops 16904999936 | tf_op jit(solution)/shard_map/close/pallas_call | solution.py:746
  121.9 2.0 %collective-permute-start.28 = (bf16[4,32,896]{2,1,0:T(8,128)(2,1)S(1)}, bf16[4,32,896]{2,1,0:T(8,128)(2,1)S(1)}, u32[]{:S(2)}, u32[]{:S(2)}) collective-permute-start(bf16[4,32,896]{2,1,0:T(8,128)(2,1)S(1)} %get-tuple-element.159), channel_id=1, source_target_pairs={{0,6},{1,7},{2,4},{3,5},{4,2},{5,3},{6,0},{7,1},{8,14},{9,15},{10,... | collective-permute-start | bytes 688136 | tf_op jit(solution)/shard_map/ppermute | solution.py:759
  127.3 5.5 %collective-permute-done.27.refs_2_ = bf16[4,32,896]{2,1,0:T(8,128)(2,1)S(1)} collective-permute-done((bf16[4,32,896]{2,1,0:T(8,128)(2,1)S(1)}, bf16[4,32,896]{2,1,0:T(8,128)(2,1)S(1)}, u32[]{:S(2)}, u32[]{:S(2)}) %collective-permute-start.27) | collective-permute-done | bytes 229408 | tf_op jit(solution)/shard_map/ppermute | solution.py:759
  132.8 2.6 %collective-permute-start.36 = (bf16[144,512]{1,0:T(8,128)(2,1)S(1)}, bf16[144,512]{1,0:T(8,128)(2,1)S(1)}, u32[]{:S(2)}, u32[]{:S(2)}) collective-permute-start(bf16[144,512]{1,0:T(8,128)(2,1)S(1)} %get-tuple-element.171), channel_id=1, source_target_pairs={{0,24},{1,25},{2,26},{3,27},{4,28},{5,29},{6,30},{7,31},{8,16},{9,... | collective-permute-start | bytes 442376 | tf_op jit(solution)/shard_map/ppermute | solution.py:759
  137.4 2.6 %collective-permute-start.33 = (bf16[32,896]{1,0:T(8,128)(2,1)S(1)}, bf16[32,896]{1,0:T(8,128)(2,1)S(1)}, u32[]{:S(2)}, u32[]{:S(2)}) collective-permute-start(bf16[32,896]{1,0:T(8,128)(2,1)S(1)} %get-tuple-element.168), channel_id=1, source_target_pairs={{0,24},{1,25},{2,26},{3,27},{4,28},{5,29},{6,30},{7,31},{8,16},{9,... | collective-permute-start | bytes 172040 | tf_op jit(solution)/shard_map/ppermute | solution.py:759
  142.3 2.3 %input_grad.1 = (f32[3,256,512]{2,1,0:T(8,128)}, f32[8,128]{1,0:T(8,128)S(1)}) custom-call(bf16[3,256,512]{2,1,0:T(8,128)(2,1)S(1)} %copy-done.2, f32[3,256,512]{2,1,0:T(8,128)S(1)} %get-tuple-element.128.refs_1_, f32[3,256,512]{2,1,0:T(8,128)S(1)} %get-tuple-element.154.refs_4_.refs_2_, bf16[3,256,512]{2,1,0:T(8,128)(2,1)S(1)} %collective-permute-done.25.refs_5_.refs_3_, ...), custom_call_target="tpu_custom_call" | custom-call | flops 345000000 | tf_op jit(solution)/shard_map/input_grad/pallas_call | solution.py:746
  (128 shorter events, 42.5 us)
Async XLA Ops:
  0.7 10.2 %collective-permute-start = (bf16[3,256,512]{2,1,0:T(8,128)(2,1)}, bf16[3,256,512]{2,1,0:T(8,128)(2,1)S(1)}, u32[]{:S(2)}, u32[]{:S(2)}) collective-permute-start(bf16[3,256,512]{2,1,0:T(8,128)(2,1)} %refs_0_.1), channel_id=1, source_target_pairs={{0,1},{1,0},{2,3},{3,2},{4,5},{5,4},{6,7},{7,6},{8,9},{9,8},{10,11... | collective-permute-start | bytes 2359304 | tf_op jit(solution)/shard_map/ppermute | solution.py:759
  5.5 12.1 %collective-permute-start.2 = (bf16[2,16,896]{2,1,0:T(8,128)(2,1)S(1)}, bf16[2,16,896]{2,1,0:T(8,128)(2,1)S(1)}, u32[]{:S(2)}, u32[]{:S(2)}) collective-permute-start(bf16[2,16,896]{2,1,0:T(8,128)(2,1)S(1)} %join.3.refs_1_), channel_id=1, source_target_pairs={{0,8},{1,9},{2,10},{3,11},{4,12},{5,13},{6,14},{7,15},{8,0},{9,1},... | collective-permute-start | bytes 172040 | tf_op jit(solution)/shard_map/ppermute | solution.py:759
  8.3 9.4 %collective-permute-start.3 = (bf16[2,16,896]{2,1,0:T(8,128)(2,1)S(1)}, bf16[2,16,896]{2,1,0:T(8,128)(2,1)S(1)}, u32[]{:S(2)}, u32[]{:S(2)}) collective-permute-start(bf16[2,16,896]{2,1,0:T(8,128)(2,1)S(1)} %join.3.refs_1_), channel_id=1, source_target_pairs={{0,16},{1,17},{2,18},{3,19},{4,20},{5,21},{6,22},{7,23},{8,24},{9,... | collective-permute-start | bytes 172040 | tf_op jit(solution)/shard_map/ppermute | solution.py:759
  18.5 16.7 %collective-permute-start.5 = (bf16[4,2,16,896]{3,2,1,0:T(8,128)(2,1)S(1)}, bf16[4,2,16,896]{3,2,1,0:T(8,128)(2,1)S(1)}, u32[]{:S(2)}, u32[]{:S(2)}) collective-permute-start(bf16[4,2,16,896]{3,2,1,0:T(8,128)(2,1)S(1)} %join.4.refs_2_.refs_5_), channel_id=1, source_target_pairs={{0,4},{1,5},{2,6},{3,7},{4,0},{5,1},{6,2},{7,3},{8,12},{9,13},{10,... | collective-permute-start | bytes 688136 | tf_op jit(solution)/shard_map/ppermute | solution.py:759
  20.1 15.2 %collective-permute-start.6 = (bf16[4,2,16,896]{3,2,1,0:T(8,128)(2,1)S(1)}, bf16[4,2,16,896]{3,2,1,0:T(8,128)(2,1)S(1)}, u32[]{:S(2)}, u32[]{:S(2)}) collective-permute-start(bf16[4,2,16,896]{3,2,1,0:T(8,128)(2,1)S(1)} %join.4.refs_2_.refs_5_), channel_id=1, source_target_pairs={{0,2},{1,3},{2,0},{3,1},{4,6},{5,7},{6,4},{7,5},{8,10},{9,11},{10,... | collective-permute-start | bytes 688136 | tf_op jit(solution)/shard_map/ppermute | solution.py:759
  21.6 13.7 %collective-permute-start.7 = (bf16[4,2,16,896]{3,2,1,0:T(8,128)(2,1)S(1)}, bf16[4,2,16,896]{3,2,1,0:T(8,128)(2,1)S(1)}, u32[]{:S(2)}, u32[]{:S(2)}) collective-permute-start(bf16[4,2,16,896]{3,2,1,0:T(8,128)(2,1)S(1)} %join.4.refs_2_.refs_5_), channel_id=1, source_target_pairs={{0,6},{1,7},{2,4},{3,5},{4,2},{5,3},{6,0},{7,1},{8,14},{9,15},{10,... | collective-permute-start | bytes 688136 | tf_op jit(solution)/shard_map/ppermute | solution.py:759
  32.2 21.4 %collective-permute-start.11 = (bf16[4,144,512]{2,1,0:T(8,128)(2,1)S(1)}, bf16[4,144,512]{2,1,0:T(8,128)(2,1)S(1)}, u32[]{:S(2)}, u32[]{:S(2)}) collective-permute-start(bf16[4,144,512]{2,1,0:T(8,128)(2,1)S(1)} %join.5.refs_0_), channel_id=1, source_target_pairs={{0,4},{1,5},{2,6},{3,7},{4,0},{5,1},{6,2},{7,3},{8,12},{9,13},{10,... | collective-permute-start | bytes 1769480 | tf_op jit(solution)/shard_map/ppermute | solution.py:759
  33.7 19.8 %collective-permute-start.12 = (bf16[4,144,512]{2,1,0:T(8,128)(2,1)S(1)}, bf16[4,144,512]{2,1,0:T(8,128)(2,1)S(1)}, u32[]{:S(2)}, u32[]{:S(2)}) collective-permute-start(bf16[4,144,512]{2,1,0:T(8,128)(2,1)S(1)} %join.5.refs_0_), channel_id=1, source_target_pairs={{0,2},{1,3},{2,0},{3,1},{4,6},{5,7},{6,4},{7,5},{8,10},{9,11},{10,... | collective-permute-start | bytes 1769480 | tf_op jit(solution)/shard_map/ppermute | solution.py:759
  44.2 9.4 %collective-permute-start.13 = (bf16[7,128,128]{2,1,0:T(8,128)(2,1)S(1)}, bf16[7,128,128]{2,1,0:T(8,128)(2,1)S(1)}, u32[]{:S(2)}, u32[]{:S(2)}) collective-permute-start(bf16[7,128,128]{2,1,0:T(8,128)(2,1)S(1)} %get-tuple-element.104), channel_id=1, source_target_pairs={{0,2},{1,3},{4,6},{5,7},{8,10},{9,11},{12,14},{13,15},{16,18},{17,... | collective-permute-start | bytes 688136 | tf_op jit(solution)/shard_map/ppermute | solution.py:899
  54.1 12.5 %collective-permute-start.17 = (bf16[12,144,512]{2,1,0:T(8,128)(2,1)S(1)}, bf16[12,144,512]{2,1,0:T(8,128)(2,1)S(1)}, u32[]{:S(2)}, u32[]{:S(2)}) collective-permute-start(bf16[12,144,512]{2,1,0:T(8,128)(2,1)S(1)} %near.1.refs_7_.refs_4_), channel_id=1, source_target_pairs={{0,1},{1,0},{2,3},{3,2},{4,5},{5,4},{6,7},{7,6},{8,9},{9,8},{10,11... | collective-permute-start | bytes 5308424 | tf_op jit(solution)/shard_map/ppermute | solution.py:759
  54.2 9.4 %collective-permute-start.14 = (bf16[2,144,512]{2,1,0:T(8,128)(2,1)S(1)}, bf16[2,144,512]{2,1,0:T(8,128)(2,1)S(1)}, u32[]{:S(2)}, u32[]{:S(2)}) collective-permute-start(bf16[2,144,512]{2,1,0:T(8,128)(2,1)S(1)} %get-tuple-element.114.refs_3_.refs_7_), channel_id=1, source_target_pairs={{0,2},{1,3},{2,0},{3,1},{4,6},{5,7},{6,4},{7,5},{8,10},{9,11},{10,... | collective-permute-start | bytes 884744 | tf_op jit(solution)/shard_map/ppermute | solution.py:759
  54.3 9.3 %collective-permute-start.15 = (bf16[2,144,512]{2,1,0:T(8,128)(2,1)S(1)}, bf16[2,144,512]{2,1,0:T(8,128)(2,1)S(1)}, u32[]{:S(2)}, u32[]{:S(2)}) collective-permute-start(bf16[2,144,512]{2,1,0:T(8,128)(2,1)S(1)} %get-tuple-element.115), channel_id=1, source_target_pairs={{0,4},{1,5},{2,6},{3,7},{4,0},{5,1},{6,2},{7,3},{8,12},{9,13},{10,... | collective-permute-start | bytes 884744 | tf_op jit(solution)/shard_map/ppermute | solution.py:759
  74.5 11.2 %collective-permute-start.20 = (bf16[2,2,4,128,512]{4,3,2,1,0:T(8,128)(2,1)S(1)}, bf16[2,2,4,128,512]{4,3,2,1,0:T(8,128)(2,1)S(1)}, u32[]{:S(2)}, u32[]{:S(2)}) collective-permute-start(bf16[2,2,4,128,512]{4,3,2,1,0:T(8,128)(2,1)S(1)} %get-tuple-element.136), channel_id=1, source_target_pairs={{0,1},{1,0},{2,3},{3,2},{4,5},{5,4},{6,7},{7,6},{8,9},{9,8},{10,11... | collective-permute-start | bytes 6291464 | tf_op jit(solution)/shard_map/ppermute | solution.py:759
  86.2 15.7 %collective-permute-start.23 = (bf16[2,2,144,512]{3,2,1,0:T(8,128)(2,1)S(1)}, bf16[2,2,144,512]{3,2,1,0:T(8,128)(2,1)S(1)}, u32[]{:S(2)}, u32[]{:S(2)}) collective-permute-start(bf16[2,2,144,512]{3,2,1,0:T(8,128)(2,1)S(1)} %get-tuple-element.150), channel_id=1, source_target_pairs={{0,4},{1,5},{2,6},{3,7},{4,0},{5,1},{6,2},{7,3},{8,12},{9,13},{10,... | collective-permute-start | bytes 1769480 | tf_op jit(solution)/shard_map/ppermute | solution.py:759
  86.9 16.2 %collective-permute-start.24 = (bf16[2,2,144,512]{3,2,1,0:T(8,128)(2,1)S(1)}, bf16[2,2,144,512]{3,2,1,0:T(8,128)(2,1)S(1)}, u32[]{:S(2)}, u32[]{:S(2)}) collective-permute-start(bf16[2,2,144,512]{3,2,1,0:T(8,128)(2,1)S(1)} %get-tuple-element.152), channel_id=1, source_target_pairs={{0,2},{1,3},{2,0},{3,1},{4,6},{5,7},{6,4},{7,5},{8,10},{9,11},{10,... | collective-permute-start | bytes 1769480 | tf_op jit(solution)/shard_map/ppermute | solution.py:759
  93.8 14.1 %collective-permute-start.22 = (bf16[7,128,128]{2,1,0:T(8,128)(2,1)S(1)}, bf16[7,128,128]{2,1,0:T(8,128)(2,1)S(1)}, u32[]{:S(2)}, u32[]{:S(2)}) collective-permute-start(bf16[7,128,128]{2,1,0:T(8,128)(2,1)S(1)} %get-tuple-element.147), channel_id=1, source_target_pairs={{2,0},{3,1},{6,4},{7,5},{10,8},{11,9},{14,12},{15,13},{18,16},{19,... | collective-permute-start | bytes 688136 | tf_op jit(solution)/shard_map/ppermute | solution.py:1020
  103.3 18.6 %collective-permute-start.29 = (bf16[2,144,512]{2,1,0:T(8,128)(2,1)S(1)}, bf16[2,144,512]{2,1,0:T(8,128)(2,1)S(1)}, u32[]{:S(2)}, u32[]{:S(2)}) collective-permute-start(bf16[2,144,512]{2,1,0:T(8,128)(2,1)S(1)} %get-tuple-element.160), channel_id=1, source_target_pairs={{0,2},{1,3},{2,0},{3,1},{4,6},{5,7},{6,4},{7,5},{8,10},{9,11},{10,... | collective-permute-start | bytes 884744 | tf_op jit(solution)/shard_map/ppermute | solution.py:759
  104.2 19.7 %collective-permute-start.30 = (bf16[2,144,512]{2,1,0:T(8,128)(2,1)S(1)}, bf16[2,144,512]{2,1,0:T(8,128)(2,1)S(1)}, u32[]{:S(2)}, u32[]{:S(2)}) collective-permute-start(bf16[2,144,512]{2,1,0:T(8,128)(2,1)S(1)} %get-tuple-element.162), channel_id=1, source_target_pairs={{0,4},{1,5},{2,6},{3,7},{4,0},{5,1},{6,2},{7,3},{8,12},{9,13},{10,... | collective-permute-start | bytes 884744 | tf_op jit(solution)/shard_map/ppermute | solution.py:759
  121.9 10.9 %collective-permute-start.27 = (bf16[4,32,896]{2,1,0:T(8,128)(2,1)S(1)}, bf16[4,32,896]{2,1,0:T(8,128)(2,1)S(1)}, u32[]{:S(2)}, u32[]{:S(2)}) collective-permute-start(bf16[4,32,896]{2,1,0:T(8,128)(2,1)S(1)} %get-tuple-element.158), channel_id=1, source_target_pairs={{0,2},{1,3},{2,0},{3,1},{4,6},{5,7},{6,4},{7,5},{8,10},{9,11},{10,... | collective-permute-start | bytes 688136 | tf_op jit(solution)/shard_map/ppermute | solution.py:759
  121.9 13.6 %collective-permute-start.25 = (bf16[3,256,512]{2,1,0:T(8,128)(2,1)S(1)}, bf16[3,256,512]{2,1,0:T(8,128)(2,1)S(1)}, u32[]{:S(2)}, u32[]{:S(2)}) collective-permute-start(bf16[3,256,512]{2,1,0:T(8,128)(2,1)S(1)} %get-tuple-element.155), channel_id=1, source_target_pairs={{0,1},{1,0},{2,3},{3,2},{4,5},{5,4},{6,7},{7,6},{8,9},{9,8},{10,11... | collective-permute-start | bytes 2359304 | tf_op jit(solution)/shard_map/ppermute | solution.py:759
  121.9 13.6 %collective-permute-start.28 = (bf16[4,32,896]{2,1,0:T(8,128)(2,1)S(1)}, bf16[4,32,896]{2,1,0:T(8,128)(2,1)S(1)}, u32[]{:S(2)}, u32[]{:S(2)}) collective-permute-start(bf16[4,32,896]{2,1,0:T(8,128)(2,1)S(1)} %get-tuple-element.159), channel_id=1, source_target_pairs={{0,6},{1,7},{2,4},{3,5},{4,2},{5,3},{6,0},{7,1},{8,14},{9,15},{10,... | collective-permute-start | bytes 688136 | tf_op jit(solution)/shard_map/ppermute | solution.py:759
  124.0 13.4 %collective-permute-start.34 = (bf16[144,512]{1,0:T(8,128)(2,1)S(1)}, bf16[144,512]{1,0:T(8,128)(2,1)S(1)}, u32[]{:S(2)}, u32[]{:S(2)}) collective-permute-start(bf16[144,512]{1,0:T(8,128)(2,1)S(1)} %get-tuple-element.169), channel_id=1, source_target_pairs={{0,8},{1,9},{2,10},{3,11},{4,12},{5,13},{6,14},{7,15},{8,0},{9,1},... | collective-permute-start | bytes 442376 | tf_op jit(solution)/shard_map/ppermute | solution.py:759
  126.4 15.1 %collective-permute-start.35 = (bf16[144,512]{1,0:T(8,128)(2,1)S(1)}, bf16[144,512]{1,0:T(8,128)(2,1)S(1)}, u32[]{:S(2)}, u32[]{:S(2)}) collective-permute-start(bf16[144,512]{1,0:T(8,128)(2,1)S(1)} %get-tuple-element.170), channel_id=1, source_target_pairs={{0,16},{1,17},{2,18},{3,19},{4,20},{5,21},{6,22},{7,23},{8,24},{9,... | collective-permute-start | bytes 442376 | tf_op jit(solution)/shard_map/ppermute | solution.py:759
  135.7 9.4 %collective-permute-start.32 = (bf16[32,896]{1,0:T(8,128)(2,1)S(1)}, bf16[32,896]{1,0:T(8,128)(2,1)S(1)}, u32[]{:S(2)}, u32[]{:S(2)}) collective-permute-start(bf16[32,896]{1,0:T(8,128)(2,1)S(1)} %get-tuple-element.167), channel_id=1, source_target_pairs={{0,16},{1,17},{2,18},{3,19},{4,20},{5,21},{6,22},{7,23},{8,24},{9,... | collective-permute-start | bytes 172040 | tf_op jit(solution)/shard_map/ppermute | solution.py:759
  (30 other events, 141.2 us)
where the time goes:
time: 149 us; the launch traced here: 148 us
  Pallas kernels  72.6 us (49%)
  starting transfers between devices  41.6 us (28%)
  waiting for transfers between devices  29.9 us (20%)
  local copies, waits for them, and re-layouts  1.85 us (1%)
    pallas_call x27, Pallas kernels, call(): pl.pallas_call(run, in_specs=[spec(kind) for kind in kinds], out_specs=[s...  72.6 us
    ppermute x36, starting transfers between devices, xor_with(): return lax.ppermute(a, BOTH, [(i, i ^ mask) for i in range(count)])  37.9 us
    ppermute x36, waiting for transfers between devices, xor_with(): return lax.ppermute(a, BOTH, [(i, i ^ mask) for i in range(count)])  27.7 us
  transfers between devices with their start and end apart: 38, of which 14 were waited for; matrix products, arithmetic and copies ran while one was open for 1% of the time, Pallas kernels for 42%

commit v1 on v0

--- a/solution.py
+++ b/solution.py
@@ -903,7 +903,7 @@
     (o_loc,) = call(
         local_kernel, seqs,
         [("s", fq), ("s", fk), ("s", fql), ("s", fkl), ("s", va), ("s", ccol), ("s", crow)],
-        [("s", feats, F32)], us=0.3, name="local",
+        [("s", feats, F32)], us=0.3, name="local", unroll=True,
     )
     if direct:
         half_z = nz // 2
@@ -1063,7 +1063,7 @@
             mix_sum_kernel, 0, [("w", a) for a in m_parts] + [("d", pause([g_line[0]], 40)), ("d", gn_recv)],
             [("w", (32, 896), BF16)] * nz, us=0.4, name="mix_sum",
         )
-        input_grad, input_done = finish_input([m_plane[0]])
+        input_grad, input_done = finish_input([g_line[0]])
         g_parts = [g_line[0]] + [xor_with(g_line[m], 8 * m, count) for m in range(1, nz)]
         up_grad, down_back, out_grad, feed_done = call(
             feed_last_kernel, 0, [("w", a) for a in g_parts],

time: 149 us -> 149 us (level)
  no operation moved by 1% of the time
where the time goes in v1:
time: 149 us; the launch traced here: 148 us
  Pallas kernels  72.2 us (48%)
  starting transfers between devices  42.5 us (29%)
  waiting for transfers between devices  29.5 us (20%)
  local copies, waits for them, and re-layouts  1.85 us (1%)
    pallas_call x27, Pallas kernels, call(): pl.pallas_call(run, in_specs=[spec(kind) for kind in kinds], out_specs=[s...  72.2 us
    ppermute x36, starting transfers between devices, xor_with(): return lax.ppermute(a, BOTH, [(i, i ^ mask) for i in range(count)])  38.8 us
    ppermute x36, waiting for transfers between devices, xor_with(): return lax.ppermute(a, BOTH, [(i, i ^ mask) for i in range(count)])  27.3 us
  transfers between devices with their start and end apart: 38, of which 14 were waited for; matrix products, arithmetic and copies ran while one was open for 1% of the time, Pallas kernels for 42%

profile of v1, /device:TPU:0, one launch (start us, length us, event | category | flops | bytes accessed | tf_op | source)
XLA Modules:
  0.0 148.3 jit_solution(4385663343076281619)
XLA Ops:
  5.5 2.8 %collective-permute-start.2 = (bf16[2,16,896]{2,1,0:T(8,128)(2,1)S(1)}, bf16[2,16,896]{2,1,0:T(8,128)(2,1)S(1)}, u32[]{:S(2)}, u32[]{:S(2)}) collective-permute-start(bf16[2,16,896]{2,1,0:T(8,128)(2,1)S(1)} %join.3.refs_1_), channel_id=1, source_target_pairs={{0,8},{1,9},{2,10},{3,11},{4,12},{5,13},{6,14},{7,15},{8,0},{9,1},... | collective-permute-start | bytes 172040 | tf_op jit(solution)/shard_map/ppermute | solution.py:759
  8.3 2.6 %collective-permute-start.3 = (bf16[2,16,896]{2,1,0:T(8,128)(2,1)S(1)}, bf16[2,16,896]{2,1,0:T(8,128)(2,1)S(1)}, u32[]{:S(2)}, u32[]{:S(2)}) collective-permute-start(bf16[2,16,896]{2,1,0:T(8,128)(2,1)S(1)} %join.3.refs_1_), channel_id=1, source_target_pairs={{0,16},{1,17},{2,18},{3,19},{4,20},{5,21},{6,22},{7,23},{8,24},{9,... | collective-permute-start | bytes 172040 | tf_op jit(solution)/shard_map/ppermute | solution.py:759
  10.9 1.9 %prepare.1 = (f32[3,512,512]{2,1,0:T(8,128)S(1)}, bf16[3,512,256]{2,1,0:T(8,128)(2,1)S(1)}) custom-call(s32[4]{0:T(128)S(1)} %pad_add_fusion.refs_0_, bf16[3,256,512]{2,1,0:T(8,128)(2,1)S(1)} %copy-done.2, bf16[3,256,512]{2,1,0:T(8,128)(2,1)S(1)} %collective-permute-done.refs_2_, bf16[3,256,512]{2,1,0:T(8,128)(2,1)S(1)} %copy-done.3), custom_call_target="tpu_custom_call" | custom-call | flops 2875000064 | tf_op jit(solution)/shard_map/prepare/pallas_call | solution.py:746
  13.7 3.8 %collective-permute-start.10 = (bf16[144,512]{1,0:T(8,128)(2,1)S(1)}, bf16[144,512]{1,0:T(8,128)(2,1)S(1)}, u32[]{:S(2)}, u32[]{:S(2)}) collective-permute-start(bf16[144,512]{1,0:T(8,128)(2,1)S(1)} %hold.1.refs_1_), channel_id=1, source_target_pairs={{0,24},{1,25},{2,26},{3,27},{4,28},{5,29},{6,30},{7,31},{8,16},{9,... | collective-permute-start | bytes 442376 | tf_op jit(solution)/shard_map/ppermute | solution.py:759
  22.1 2.5 %collective-permute-start.9 = (bf16[144,512]{1,0:T(8,128)(2,1)S(1)}, bf16[144,512]{1,0:T(8,128)(2,1)S(1)}, u32[]{:S(2)}, u32[]{:S(2)}) collective-permute-start(bf16[144,512]{1,0:T(8,128)(2,1)S(1)} %hold.1.refs_1_), channel_id=1, source_target_pairs={{0,16},{1,17},{2,18},{3,19},{4,20},{5,21},{6,22},{7,23},{8,24},{9,... | collective-permute-start | bytes 442376 | tf_op jit(solution)/shard_map/ppermute | solution.py:759
  24.9 4.5 %collective-permute-done.8.refs_2_ = bf16[144,512]{1,0:T(8,128)(2,1)S(1)} collective-permute-done((bf16[144,512]{1,0:T(8,128)(2,1)S(1)}, bf16[144,512]{1,0:T(8,128)(2,1)S(1)}, u32[]{:S(2)}, u32[]{:S(2)}) %collective-permute-start.8) | collective-permute-done | bytes 147488 | tf_op jit(solution)/shard_map/ppermute | solution.py:759
  35.3 8.8 %project.1 = (bf16[3,512,512]{2,1,0:T(8,128)(2,1)S(1)}, bf16[3,4,512,128]{3,2,1,0:T(8,128)(2,1)S(1)}, bf16[3,4,512,128]{3,2,1,0:T(8,128)(2,1)S(1)}, bf16[3,4,512...) custom-call(s32[4]{0:T(128)S(1)} %pad_add_fusion.refs_0_, ...), custom_call_target="tpu_custom_call" | custom-call | flops 13799999488 | tf_op jit(solution)/shard_map/project/pallas_call | solution.py:746
  44.2 2.4 %collective-permute-start.13 = (bf16[7,128,128]{2,1,0:T(8,128)(2,1)S(1)}, bf16[7,128,128]{2,1,0:T(8,128)(2,1)S(1)}, u32[]{:S(2)}, u32[]{:S(2)}) collective-permute-start(bf16[7,128,128]{2,1,0:T(8,128)(2,1)S(1)} %get-tuple-element.104), channel_id=1, source_target_pairs={{0,2},{1,3},{4,6},{5,7},{8,10},{9,11},{12,14},{13,15},{16,18},{17,... | collective-permute-start | bytes 688136 | tf_op jit(solution)/shard_map/ppermute | solution.py:899
  46.6 3.6 %query.1 = (bf16[3,4,512,128]{3,2,1,0:T(8,128)(2,1)S(1)}, bf16[3,4,512,128]{3,2,1,0:T(8,128)(2,1)S(1)}, bf16[3,4,512,128]{3,2,1,0:T(8,128)(2,1)S(1)}) custom-call(bf16[3,512,512]{2,1,0:T(8,128)(2,1)S(1)} %get-tuple-element.105.refs_0_.refs_2_, bf16[512,896]{1,0:T(8,128)(2,1)S(1)} %get-tuple-element.106.refs_1_.refs_16_, ...), custom_call_target="tpu_custom_call" | custom-call | flops 345000000 | tf_op jit(solution)/shard_map/query/pallas_call | solution.py:746
  50.2 2.9 %local.1.refs_3_.refs_1_ = f32[3,4,512,128]{3,2,1,0:T(8,128)S(1)} custom-call(bf16[3,4,512,128]{3,2,1,0:T(8,128)(2,1)S(1)} %get-tuple-element.107.refs_0_.refs_2_.refs_5_.refs_3_, bf16[3,4,512,128]{3,2,1,0:T(8,128)(2,1)S(1)} %get-tuple-element.108.refs_1_.refs_4_, bf16[3,4,512,128]{3,2,1,0:T(8,128)(2,1)S(1)} %get-tuple-element.109.refs_2_, ...), custom_call_target="tpu_custom_call" | custom-call | flops 345000000 | tf_op jit(solution)/shard_map/local/pallas_call | solution.py:746
  54.5 4.1 %finish.1 = (f32[3,4,512,128]{3,2,1,0:T(8,128)S(1)}, f32[3,4,512,128]{3,2,1,0:T(8,128)S(1)}, bf16[3,4,2,128,128]{4,3,2,1,0:T(8,128)(2,1)S(1)}, bf16[3,256,256]{2,1,0:T(8,128)(2,1)S(1)}, bf16[3,256,256]{2,1,0:T(8,128)(2,1)S(1)}) custom-call(s32[4]{0:T(128)S(1)} %pad_add_fusion.refs_0_, f32[3,4,512,128]{3,2,1,0:T(8,128)S(1)} %local.1.refs_3_.refs_1_, ...), custom_call_target="tpu_custom_call" | custom-call | flops 345000000 | tf_op jit(solution)/shard_map/finish/pallas_call | solution.py:746
  58.6 4.6 %collective-permute-done.14.refs_0_ = bf16[2,144,512]{2,1,0:T(8,128)(2,1)S(1)} collective-permute-done((bf16[2,144,512]{2,1,0:T(8,128)(2,1)S(1)}, bf16[2,144,512]{2,1,0:T(8,128)(2,1)S(1)}, u32[]{:S(2)}, u32[]{:S(2)}) %collective-permute-start.14) | collective-permute-done | bytes 294944 | tf_op jit(solution)/shard_map/ppermute | solution.py:759
  64.1 2.1 %collective-permute-done.16.refs_2_ = bf16[3,256,256]{2,1,0:T(8,128)(2,1)S(1)} collective-permute-done((bf16[3,256,256]{2,1,0:T(8,128)(2,1)S(1)}, bf16[3,256,256]{2,1,0:T(8,128)(2,1)S(1)}, u32[]{:S(2)}, u32[]{:S(2)}) %collective-permute-start.16) | collective-permute-done | bytes 393248 | tf_op jit(solution)/shard_map/ppermute | solution.py:759
  66.2 7.9 %feed_first.1 = (bf16[2,2,4,128,512]{4,3,2,1,0:T(8,128)(2,1)S(1)}, f32[768,512]{1,0:T(8,128)S(1)}, f32[768,512]{1,0:T(8,128)S(1)}, f32[768,512]{1,0:T(8,128)S(1)...) custom-call(s32[4]{0:T(128)S(1)} %pad_add_fusion.refs_0_, ...), custom_call_target="tpu_custom_call" | custom-call | flops 11500000256 | tf_op jit(solution)/shard_map/feed_first/pallas_call | solution.py:746
  74.3 9.4 %feed_second.1 = (bf16[3,256,512]{2,1,0:T(8,128)(2,1)}, f32[3,256,512]{2,1,0:T(8,128)S(1)}, bf16[3,256,256]{2,1,0:T(8,128)(2,1)S(1)}, bf16[3,256,256]{2,1,0:T(8,...) custom-call(s32[4]{0:T(128)S(1)} %pad_add_fusion.refs_0_, ...), custom_call_target="tpu_custom_call" | custom-call | flops 11500000256 | tf_op jit(solution)/shard_map/feed_second/pallas_call | solution.py:746
  88.2 5.2 %adjoint.1 = (bf16[3,4,512,128]{3,2,1,0:T(8,128)(2,1)S(1)}, bf16[3,4,512,128]{3,2,1,0:T(8,128)(2,1)S(1)}, f32[3,4,128,128]{3,2,1,0:T(8,128)S(1)}, bf16[7,128,128]{2,1,0:T(8,128)(2,1)S(1)}) custom-call(s32[4]{0:T(128)S(1)} %pad_add_fusion.refs_0_, bf16[3,256,256]{2,1,0:T(8,128)(2,1)S(1)} %get-tuple-element.131.refs_1_, ...), custom_call_target="tpu_custom_call" | custom-call | flops 345000000 | tf_op jit(solution)/shard_map/adjoint/pallas_call | solution.py:746
  94.8 5.3 %local_back.1 = (f32[3,4,512,128]{3,2,1,0:T(8,128)S(1)}, f32[3,4,512,128]{3,2,1,0:T(8,128)S(1)}, f32[3,4,512,128]{3,2,1,0:T(8,128)S(1)}) custom-call(bf16[3,4,512,128]{3,2,1,0:T(8,128)(2,1)S(1)} %get-tuple-element.107.refs_0_.refs_2_.refs_5_.refs_3_, bf16[3,4,512,128]{3,2,1,0:T(8,128)(2,1)S(1)} %get-tuple-element.108.refs_1_.refs_4_, ...), custom_call_target="tpu_custom_call" | custom-call | flops 345000000 | tf_op jit(solution)/shard_map/local_back/pallas_call | solution.py:746
  105.3 2.2 %collective-permute-done.22.refs_13_ = bf16[7,128,128]{2,1,0:T(8,128)(2,1)S(1)} collective-permute-done((bf16[7,128,128]{2,1,0:T(8,128)(2,1)S(1)}, bf16[7,128,128]{2,1,0:T(8,128)(2,1)S(1)}, u32[]{:S(2)}, u32[]{:S(2)}) %collective-permute-start.22) | collective-permute-done | bytes 229408 | tf_op jit(solution)/shard_map/ppermute | solution.py:1020
  107.6 12.4 %close.1 = (bf16[4,32,896]{2,1,0:T(8,128)(2,1)S(1)}, bf16[4,32,896]{2,1,0:T(8,128)(2,1)S(1)}, bf16[4,32,896]{2,1,0:T(8,128)(2,1)S(1)}, bf16[4,32,896]{2,1,0:T(8,...) custom-call(s32[4]{0:T(128)S(1)} %pad_add_fusion.refs_0_, f32[3,512,512]{2,1,0:T(8,128)S(1)} %copy-done.7, ...), custom_call_target="tpu_custom_call" | custom-call | flops 16904999936 | tf_op jit(solution)/shard_map/close/pallas_call | solution.py:746
  121.5 2.0 %collective-permute-start.30 = (bf16[4,32,896]{2,1,0:T(8,128)(2,1)S(1)}, bf16[4,32,896]{2,1,0:T(8,128)(2,1)S(1)}, u32[]{:S(2)}, u32[]{:S(2)}) collective-permute-start(bf16[4,32,896]{2,1,0:T(8,128)(2,1)S(1)} %get-tuple-element.164), channel_id=1, source_target_pairs={{0,6},{1,7},{2,4},{3,5},{4,2},{5,3},{6,0},{7,1},{8,14},{9,15},{10,... | collective-permute-start | bytes 688136 | tf_op jit(solution)/shard_map/ppermute | solution.py:759
  127.3 5.1 %collective-permute-done.29.refs_2_ = bf16[4,32,896]{2,1,0:T(8,128)(2,1)S(1)} collective-permute-done((bf16[4,32,896]{2,1,0:T(8,128)(2,1)S(1)}, bf16[4,32,896]{2,1,0:T(8,128)(2,1)S(1)}, u32[]{:S(2)}, u32[]{:S(2)}) %collective-permute-start.29) | collective-permute-done | bytes 229408 | tf_op jit(solution)/shard_map/ppermute | solution.py:759
  132.4 3.0 %collective-permute-start.36 = (bf16[144,512]{1,0:T(8,128)(2,1)S(1)}, bf16[144,512]{1,0:T(8,128)(2,1)S(1)}, u32[]{:S(2)}, u32[]{:S(2)}) collective-permute-start(bf16[144,512]{1,0:T(8,128)(2,1)S(1)} %get-tuple-element.171), channel_id=1, source_target_pairs={{0,24},{1,25},{2,26},{3,27},{4,28},{5,29},{6,30},{7,31},{8,16},{9,... | collective-permute-start | bytes 442376 | tf_op jit(solution)/shard_map/ppermute | solution.py:759
  137.0 3.0 %collective-permute-start.33 = (bf16[32,896]{1,0:T(8,128)(2,1)S(1)}, bf16[32,896]{1,0:T(8,128)(2,1)S(1)}, u32[]{:S(2)}, u32[]{:S(2)}) collective-permute-start(bf16[32,896]{1,0:T(8,128)(2,1)S(1)} %get-tuple-element.168), channel_id=1, source_target_pairs={{0,24},{1,25},{2,26},{3,27},{4,28},{5,29},{6,30},{7,31},{8,16},{9,... | collective-permute-start | bytes 172040 | tf_op jit(solution)/shard_map/ppermute | solution.py:759
  142.0 2.3 %input_grad.1 = (f32[3,256,512]{2,1,0:T(8,128)}, f32[8,128]{1,0:T(8,128)S(1)}) custom-call(bf16[3,256,512]{2,1,0:T(8,128)(2,1)S(1)} %copy-done.2, f32[3,256,512]{2,1,0:T(8,128)S(1)} %get-tuple-element.128.refs_1_, f32[3,256,512]{2,1,0:T(8,128)S(1)} %get-tuple-element.154.refs_4_.refs_2_, bf16[3,256,512]{2,1,0:T(8,128)(2,1)S(1)} %collective-permute-done.25.refs_3_.refs_5_, ...), custom_call_target="tpu_custom_call" | custom-call | flops 345000000 | tf_op jit(solution)/shard_map/input_grad/pallas_call | solution.py:746
  (128 shorter events, 42.6 us)
Async XLA Ops:
  0.7 10.2 %collective-permute-start = (bf16[3,256,512]{2,1,0:T(8,128)(2,1)}, bf16[3,256,512]{2,1,0:T(8,128)(2,1)S(1)}, u32[]{:S(2)}, u32[]{:S(2)}) collective-permute-start(bf16[3,256,512]{2,1,0:T(8,128)(2,1)} %refs_0_.1), channel_id=1, source_target_pairs={{0,1},{1,0},{2,3},{3,2},{4,5},{5,4},{6,7},{7,6},{8,9},{9,8},{10,11... | collective-permute-start | bytes 2359304 | tf_op jit(solution)/shard_map/ppermute | solution.py:759
  5.5 12.1 %collective-permute-start.2 = (bf16[2,16,896]{2,1,0:T(8,128)(2,1)S(1)}, bf16[2,16,896]{2,1,0:T(8,128)(2,1)S(1)}, u32[]{:S(2)}, u32[]{:S(2)}) collective-permute-start(bf16[2,16,896]{2,1,0:T(8,128)(2,1)S(1)} %join.3.refs_1_), channel_id=1, source_target_pairs={{0,8},{1,9},{2,10},{3,11},{4,12},{5,13},{6,14},{7,15},{8,0},{9,1},... | collective-permute-start | bytes 172040 | tf_op jit(solution)/shard_map/ppermute | solution.py:759
  8.3 9.4 %collective-permute-start.3 = (bf16[2,16,896]{2,1,0:T(8,128)(2,1)S(1)}, bf16[2,16,896]{2,1,0:T(8,128)(2,1)S(1)}, u32[]{:S(2)}, u32[]{:S(2)}) collective-permute-start(bf16[2,16,896]{2,1,0:T(8,128)(2,1)S(1)} %join.3.refs_1_), channel_id=1, source_target_pairs={{0,16},{1,17},{2,18},{3,19},{4,20},{5,21},{6,22},{7,23},{8,24},{9,... | collective-permute-start | bytes 172040 | tf_op jit(solution)/shard_map/ppermute | solution.py:759
  18.5 16.7 %collective-permute-start.5 = (bf16[4,2,16,896]{3,2,1,0:T(8,128)(2,1)S(1)}, bf16[4,2,16,896]{3,2,1,0:T(8,128)(2,1)S(1)}, u32[]{:S(2)}, u32[]{:S(2)}) collective-permute-start(bf16[4,2,16,896]{3,2,1,0:T(8,128)(2,1)S(1)} %join.4.refs_2_.refs_5_), channel_id=1, source_target_pairs={{0,4},{1,5},{2,6},{3,7},{4,0},{5,1},{6,2},{7,3},{8,12},{9,13},{10,... | collective-permute-start | bytes 688136 | tf_op jit(solution)/shard_map/ppermute | solution.py:759
  20.1 15.2 %collective-permute-start.6 = (bf16[4,2,16,896]{3,2,1,0:T(8,128)(2,1)S(1)}, bf16[4,2,16,896]{3,2,1,0:T(8,128)(2,1)S(1)}, u32[]{:S(2)}, u32[]{:S(2)}) collective-permute-start(bf16[4,2,16,896]{3,2,1,0:T(8,128)(2,1)S(1)} %join.4.refs_2_.refs_5_), channel_id=1, source_target_pairs={{0,2},{1,3},{2,0},{3,1},{4,6},{5,7},{6,4},{7,5},{8,10},{9,11},{10,... | collective-permute-start | bytes 688136 | tf_op jit(solution)/shard_map/ppermute | solution.py:759
  21.6 13.7 %collective-permute-start.7 = (bf16[4,2,16,896]{3,2,1,0:T(8,128)(2,1)S(1)}, bf16[4,2,16,896]{3,2,1,0:T(8,128)(2,1)S(1)}, u32[]{:S(2)}, u32[]{:S(2)}) collective-permute-start(bf16[4,2,16,896]{3,2,1,0:T(8,128)(2,1)S(1)} %join.4.refs_2_.refs_5_), channel_id=1, source_target_pairs={{0,6},{1,7},{2,4},{3,5},{4,2},{5,3},{6,0},{7,1},{8,14},{9,15},{10,... | collective-permute-start | bytes 688136 | tf_op jit(solution)/shard_map/ppermute | solution.py:759
  32.2 21.0 %collective-permute-start.11 = (bf16[4,144,512]{2,1,0:T(8,128)(2,1)S(1)}, bf16[4,144,512]{2,1,0:T(8,128)(2,1)S(1)}, u32[]{:S(2)}, u32[]{:S(2)}) collective-permute-start(bf16[4,144,512]{2,1,0:T(8,128)(2,1)S(1)} %join.5.refs_0_), channel_id=1, source_target_pairs={{0,4},{1,5},{2,6},{3,7},{4,0},{5,1},{6,2},{7,3},{8,12},{9,13},{10,... | collective-permute-start | bytes 1769480 | tf_op jit(solution)/shard_map/ppermute | solution.py:759
  33.7 19.4 %collective-permute-start.12 = (bf16[4,144,512]{2,1,0:T(8,128)(2,1)S(1)}, bf16[4,144,512]{2,1,0:T(8,128)(2,1)S(1)}, u32[]{:S(2)}, u32[]{:S(2)}) collective-permute-start(bf16[4,144,512]{2,1,0:T(8,128)(2,1)S(1)} %join.5.refs_0_), channel_id=1, source_target_pairs={{0,2},{1,3},{2,0},{3,1},{4,6},{5,7},{6,4},{7,5},{8,10},{9,11},{10,... | collective-permute-start | bytes 1769480 | tf_op jit(solution)/shard_map/ppermute | solution.py:759
  44.2 9.0 %collective-permute-start.13 = (bf16[7,128,128]{2,1,0:T(8,128)(2,1)S(1)}, bf16[7,128,128]{2,1,0:T(8,128)(2,1)S(1)}, u32[]{:S(2)}, u32[]{:S(2)}) collective-permute-start(bf16[7,128,128]{2,1,0:T(8,128)(2,1)S(1)} %get-tuple-element.104), channel_id=1, source_target_pairs={{0,2},{1,3},{4,6},{5,7},{8,10},{9,11},{12,14},{13,15},{16,18},{17,... | collective-permute-start | bytes 688136 | tf_op jit(solution)/shard_map/ppermute | solution.py:899
  53.7 12.5 %collective-permute-start.17 = (bf16[12,144,512]{2,1,0:T(8,128)(2,1)S(1)}, bf16[12,144,512]{2,1,0:T(8,128)(2,1)S(1)}, u32[]{:S(2)}, u32[]{:S(2)}) collective-permute-start(bf16[12,144,512]{2,1,0:T(8,128)(2,1)S(1)} %near.1.refs_7_.refs_4_), channel_id=1, source_target_pairs={{0,1},{1,0},{2,3},{3,2},{4,5},{5,4},{6,7},{7,6},{8,9},{9,8},{10,11... | collective-permute-start | bytes 5308424 | tf_op jit(solution)/shard_map/ppermute | solution.py:759
  53.8 9.4 %collective-permute-start.14 = (bf16[2,144,512]{2,1,0:T(8,128)(2,1)S(1)}, bf16[2,144,512]{2,1,0:T(8,128)(2,1)S(1)}, u32[]{:S(2)}, u32[]{:S(2)}) collective-permute-start(bf16[2,144,512]{2,1,0:T(8,128)(2,1)S(1)} %get-tuple-element.114.refs_3_.refs_7_), channel_id=1, source_target_pairs={{0,2},{1,3},{2,0},{3,1},{4,6},{5,7},{6,4},{7,5},{8,10},{9,11},{10,... | collective-permute-start | bytes 884744 | tf_op jit(solution)/shard_map/ppermute | solution.py:759
  53.9 9.3 %collective-permute-start.15 = (bf16[2,144,512]{2,1,0:T(8,128)(2,1)S(1)}, bf16[2,144,512]{2,1,0:T(8,128)(2,1)S(1)}, u32[]{:S(2)}, u32[]{:S(2)}) collective-permute-start(bf16[2,144,512]{2,1,0:T(8,128)(2,1)S(1)} %get-tuple-element.115), channel_id=1, source_target_pairs={{0,4},{1,5},{2,6},{3,7},{4,0},{5,1},{6,2},{7,3},{8,12},{9,13},{10,... | collective-permute-start | bytes 884744 | tf_op jit(solution)/shard_map/ppermute | solution.py:759
  74.1 11.2 %collective-permute-start.20 = (bf16[2,2,4,128,512]{4,3,2,1,0:T(8,128)(2,1)S(1)}, bf16[2,2,4,128,512]{4,3,2,1,0:T(8,128)(2,1)S(1)}, u32[]{:S(2)}, u32[]{:S(2)}) collective-permute-start(bf16[2,2,4,128,512]{4,3,2,1,0:T(8,128)(2,1)S(1)} %get-tuple-element.136), channel_id=1, source_target_pairs={{0,1},{1,0},{2,3},{3,2},{4,5},{5,4},{6,7},{7,6},{8,9},{9,8},{10,11... | collective-permute-start | bytes 6291464 | tf_op jit(solution)/shard_map/ppermute | solution.py:759
  85.8 15.7 %collective-permute-start.23 = (bf16[2,2,144,512]{3,2,1,0:T(8,128)(2,1)S(1)}, bf16[2,2,144,512]{3,2,1,0:T(8,128)(2,1)S(1)}, u32[]{:S(2)}, u32[]{:S(2)}) collective-permute-start(bf16[2,2,144,512]{3,2,1,0:T(8,128)(2,1)S(1)} %get-tuple-element.150), channel_id=1, source_target_pairs={{0,4},{1,5},{2,6},{3,7},{4,0},{5,1},{6,2},{7,3},{8,12},{9,13},{10,... | collective-permute-start | bytes 1769480 | tf_op jit(solution)/shard_map/ppermute | solution.py:759
  86.4 16.2 %collective-permute-start.24 = (bf16[2,2,144,512]{3,2,1,0:T(8,128)(2,1)S(1)}, bf16[2,2,144,512]{3,2,1,0:T(8,128)(2,1)S(1)}, u32[]{:S(2)}, u32[]{:S(2)}) collective-permute-start(bf16[2,2,144,512]{3,2,1,0:T(8,128)(2,1)S(1)} %get-tuple-element.152), channel_id=1, source_target_pairs={{0,2},{1,3},{2,0},{3,1},{4,6},{5,7},{6,4},{7,5},{8,10},{9,11},{10,... | collective-permute-start | bytes 1769480 | tf_op jit(solution)/shard_map/ppermute | solution.py:759
  93.4 14.1 %collective-permute-start.22 = (bf16[7,128,128]{2,1,0:T(8,128)(2,1)S(1)}, bf16[7,128,128]{2,1,0:T(8,128)(2,1)S(1)}, u32[]{:S(2)}, u32[]{:S(2)}) collective-permute-start(bf16[7,128,128]{2,1,0:T(8,128)(2,1)S(1)} %get-tuple-element.147), channel_id=1, source_target_pairs={{2,0},{3,1},{6,4},{7,5},{10,8},{11,9},{14,12},{15,13},{18,16},{19,... | collective-permute-start | bytes 688136 | tf_op jit(solution)/shard_map/ppermute | solution.py:1020
  102.9 18.6 %collective-permute-start.26 = (bf16[2,144,512]{2,1,0:T(8,128)(2,1)S(1)}, bf16[2,144,512]{2,1,0:T(8,128)(2,1)S(1)}, u32[]{:S(2)}, u32[]{:S(2)}) collective-permute-start(bf16[2,144,512]{2,1,0:T(8,128)(2,1)S(1)} %get-tuple-element.156), channel_id=1, source_target_pairs={{0,2},{1,3},{2,0},{3,1},{4,6},{5,7},{6,4},{7,5},{8,10},{9,11},{10,... | collective-permute-start | bytes 884744 | tf_op jit(solution)/shard_map/ppermute | solution.py:759
  103.8 19.6 %collective-permute-start.27 = (bf16[2,144,512]{2,1,0:T(8,128)(2,1)S(1)}, bf16[2,144,512]{2,1,0:T(8,128)(2,1)S(1)}, u32[]{:S(2)}, u32[]{:S(2)}) collective-permute-start(bf16[2,144,512]{2,1,0:T(8,128)(2,1)S(1)} %get-tuple-element.158), channel_id=1, source_target_pairs={{0,4},{1,5},{2,6},{3,7},{4,0},{5,1},{6,2},{7,3},{8,12},{9,13},{10,... | collective-permute-start | bytes 884744 | tf_op jit(solution)/shard_map/ppermute | solution.py:759
  121.5 10.9 %collective-permute-start.29 = (bf16[4,32,896]{2,1,0:T(8,128)(2,1)S(1)}, bf16[4,32,896]{2,1,0:T(8,128)(2,1)S(1)}, u32[]{:S(2)}, u32[]{:S(2)}) collective-permute-start(bf16[4,32,896]{2,1,0:T(8,128)(2,1)S(1)} %get-tuple-element.163), channel_id=1, source_target_pairs={{0,2},{1,3},{2,0},{3,1},{4,6},{5,7},{6,4},{7,5},{8,10},{9,11},{10,... | collective-permute-start | bytes 688136 | tf_op jit(solution)/shard_map/ppermute | solution.py:759
  121.5 14.0 %collective-permute-start.25 = (bf16[3,256,512]{2,1,0:T(8,128)(2,1)S(1)}, bf16[3,256,512]{2,1,0:T(8,128)(2,1)S(1)}, u32[]{:S(2)}, u32[]{:S(2)}) collective-permute-start(bf16[3,256,512]{2,1,0:T(8,128)(2,1)S(1)} %get-tuple-element.155), channel_id=1, source_target_pairs={{0,1},{1,0},{2,3},{3,2},{4,5},{5,4},{6,7},{7,6},{8,9},{9,8},{10,11... | collective-permute-start | bytes 2359304 | tf_op jit(solution)/shard_map/ppermute | solution.py:759
  121.5 14.0 %collective-permute-start.30 = (bf16[4,32,896]{2,1,0:T(8,128)(2,1)S(1)}, bf16[4,32,896]{2,1,0:T(8,128)(2,1)S(1)}, u32[]{:S(2)}, u32[]{:S(2)}) collective-permute-start(bf16[4,32,896]{2,1,0:T(8,128)(2,1)S(1)} %get-tuple-element.164), channel_id=1, source_target_pairs={{0,6},{1,7},{2,4},{3,5},{4,2},{5,3},{6,0},{7,1},{8,14},{9,15},{10,... | collective-permute-start | bytes 688136 | tf_op jit(solution)/shard_map/ppermute | solution.py:759
  123.6 13.4 %collective-permute-start.34 = (bf16[144,512]{1,0:T(8,128)(2,1)S(1)}, bf16[144,512]{1,0:T(8,128)(2,1)S(1)}, u32[]{:S(2)}, u32[]{:S(2)}) collective-permute-start(bf16[144,512]{1,0:T(8,128)(2,1)S(1)} %get-tuple-element.169), channel_id=1, source_target_pairs={{0,8},{1,9},{2,10},{3,11},{4,12},{5,13},{6,14},{7,15},{8,0},{9,1},... | collective-permute-start | bytes 442376 | tf_op jit(solution)/shard_map/ppermute | solution.py:759
  126.0 15.3 %collective-permute-start.35 = (bf16[144,512]{1,0:T(8,128)(2,1)S(1)}, bf16[144,512]{1,0:T(8,128)(2,1)S(1)}, u32[]{:S(2)}, u32[]{:S(2)}) collective-permute-start(bf16[144,512]{1,0:T(8,128)(2,1)S(1)} %get-tuple-element.170), channel_id=1, source_target_pairs={{0,16},{1,17},{2,18},{3,19},{4,20},{5,21},{6,22},{7,23},{8,24},{9,... | collective-permute-start | bytes 442376 | tf_op jit(solution)/shard_map/ppermute | solution.py:759
  135.7 9.4 %collective-permute-start.32 = (bf16[32,896]{1,0:T(8,128)(2,1)S(1)}, bf16[32,896]{1,0:T(8,128)(2,1)S(1)}, u32[]{:S(2)}, u32[]{:S(2)}) collective-permute-start(bf16[32,896]{1,0:T(8,128)(2,1)S(1)} %get-tuple-element.167), channel_id=1, source_target_pairs={{0,16},{1,17},{2,18},{3,19},{4,20},{5,21},{6,22},{7,23},{8,24},{9,... | collective-permute-start | bytes 172040 | tf_op jit(solution)/shard_map/ppermute | solution.py:759
  (30 other events, 141.2 us)

commit v2 on v1

--- a/solution.py
+++ b/solution.py
@@ -917,7 +917,7 @@
             gather_kernel, 0, [("a", a) for a in near_parts] + [("d", x_half)],
             [("w", (3 * nz, *ff_line.shape[1:]), BF16)], scratch=[pltpu.SemaphoreType.DMA((3,))], us=0.5, name="near",
         )
-        before_finish = [x_half]
+        before_finish = [x_half, ff_near]
     else:
         before_finish = []
     (inv_root, turn, st, att_keep, att_send) = call(
@@ -1060,7 +1060,7 @@
 
     if direct:
         m_plane = call(
-            mix_sum_kernel, 0, [("w", a) for a in m_parts] + [("d", pause([g_line[0]], 40)), ("d", gn_recv)],
+            mix_sum_kernel, 0, [("w", a) for a in m_parts] + [("d", pause([g_line[0]], 15)), ("d", gn_recv)],
             [("w", (32, 896), BF16)] * nz, us=0.4, name="mix_sum",
         )
         input_grad, input_done = finish_input([g_line[0]])

time: 149 us -> 149 us (level)
  no operation moved by 1% of the time
where the time goes in v2:
time: 149 us; the launch traced here: 148 us
  Pallas kernels  72.3 us (49%)
  starting transfers between devices  42.4 us (28%)
  waiting for transfers between devices  29.6 us (20%)
  local copies, waits for them, and re-layouts  1.85 us (1%)
    pallas_call x27, Pallas kernels, call(): pl.pallas_call(run, in_specs=[spec(kind) for kind in kinds], out_specs=[s...  72.3 us
    ppermute x36, starting transfers between devices, xor_with(): return lax.ppermute(a, BOTH, [(i, i ^ mask) for i in range(count)])  38.7 us
    ppermute x36, waiting for transfers between devices, xor_with(): return lax.ppermute(a, BOTH, [(i, i ^ mask) for i in range(count)])  27.3 us
  transfers between devices with their start and end apart: 38, of which 14 were waited for; matrix products, arithmetic and copies ran while one was open for 1% of the time, Pallas kernels for 42%

profile of v2, /device:TPU:0, one launch (start us, length us, event | category | flops | bytes accessed | tf_op | source)
XLA Modules:
  0.0 148.4 jit_solution(494607986040639178)
XLA Ops:
  5.5 2.8 %collective-permute-start.2 = (bf16[2,16,896]{2,1,0:T(8,128)(2,1)S(1)}, bf16[2,16,896]{2,1,0:T(8,128)(2,1)S(1)}, u32[]{:S(2)}, u32[]{:S(2)}) collective-permute-start(bf16[2,16,896]{2,1,0:T(8,128)(2,1)S(1)} %join.3.refs_1_), channel_id=1, source_target_pairs={{0,8},{1,9},{2,10},{3,11},{4,12},{5,13},{6,14},{7,15},{8,0},{9,1},... | collective-permute-start | bytes 172040 | tf_op jit(solution)/shard_map/ppermute | solution.py:759
  8.3 2.6 %collective-permute-start.3 = (bf16[2,16,896]{2,1,0:T(8,128)(2,1)S(1)}, bf16[2,16,896]{2,1,0:T(8,128)(2,1)S(1)}, u32[]{:S(2)}, u32[]{:S(2)}) collective-permute-start(bf16[2,16,896]{2,1,0:T(8,128)(2,1)S(1)} %join.3.refs_1_), channel_id=1, source_target_pairs={{0,16},{1,17},{2,18},{3,19},{4,20},{5,21},{6,22},{7,23},{8,24},{9,... | collective-permute-start | bytes 172040 | tf_op jit(solution)/shard_map/ppermute | solution.py:759
  10.9 1.9 %prepare.1 = (f32[3,512,512]{2,1,0:T(8,128)S(1)}, bf16[3,512,256]{2,1,0:T(8,128)(2,1)S(1)}) custom-call(s32[4]{0:T(128)S(1)} %pad_add_fusion.refs_0_, bf16[3,256,512]{2,1,0:T(8,128)(2,1)S(1)} %copy-done.2, bf16[3,256,512]{2,1,0:T(8,128)(2,1)S(1)} %collective-permute-done.refs_2_, bf16[3,256,512]{2,1,0:T(8,128)(2,1)S(1)} %copy-done.3), custom_call_target="tpu_custom_call" | custom-call | flops 2875000064 | tf_op jit(solution)/shard_map/prepare/pallas_call | solution.py:746
  13.7 3.8 %collective-permute-start.10 = (bf16[144,512]{1,0:T(8,128)(2,1)S(1)}, bf16[144,512]{1,0:T(8,128)(2,1)S(1)}, u32[]{:S(2)}, u32[]{:S(2)}) collective-permute-start(bf16[144,512]{1,0:T(8,128)(2,1)S(1)} %hold.1.refs_1_), channel_id=1, source_target_pairs={{0,24},{1,25},{2,26},{3,27},{4,28},{5,29},{6,30},{7,31},{8,16},{9,... | collective-permute-start | bytes 442376 | tf_op jit(solution)/shard_map/ppermute | solution.py:759
  22.1 2.5 %collective-permute-start.9 = (bf16[144,512]{1,0:T(8,128)(2,1)S(1)}, bf16[144,512]{1,0:T(8,128)(2,1)S(1)}, u32[]{:S(2)}, u32[]{:S(2)}) collective-permute-start(bf16[144,512]{1,0:T(8,128)(2,1)S(1)} %hold.1.refs_1_), channel_id=1, source_target_pairs={{0,16},{1,17},{2,18},{3,19},{4,20},{5,21},{6,22},{7,23},{8,24},{9,... | collective-permute-start | bytes 442376 | tf_op jit(solution)/shard_map/ppermute | solution.py:759
  24.9 4.5 %collective-permute-done.8.refs_2_ = bf16[144,512]{1,0:T(8,128)(2,1)S(1)} collective-permute-done((bf16[144,512]{1,0:T(8,128)(2,1)S(1)}, bf16[144,512]{1,0:T(8,128)(2,1)S(1)}, u32[]{:S(2)}, u32[]{:S(2)}) %collective-permute-start.8) | collective-permute-done | bytes 147488 | tf_op jit(solution)/shard_map/ppermute | solution.py:759
  35.3 8.8 %project.1 = (bf16[3,512,512]{2,1,0:T(8,128)(2,1)S(1)}, bf16[3,4,512,128]{3,2,1,0:T(8,128)(2,1)S(1)}, bf16[3,4,512,128]{3,2,1,0:T(8,128)(2,1)S(1)}, bf16[3,4,512...) custom-call(s32[4]{0:T(128)S(1)} %pad_add_fusion.refs_0_, ...), custom_call_target="tpu_custom_call" | custom-call | flops 13799999488 | tf_op jit(solution)/shard_map/project/pallas_call | solution.py:746
  44.2 2.4 %collective-permute-start.13 = (bf16[7,128,128]{2,1,0:T(8,128)(2,1)S(1)}, bf16[7,128,128]{2,1,0:T(8,128)(2,1)S(1)}, u32[]{:S(2)}, u32[]{:S(2)}) collective-permute-start(bf16[7,128,128]{2,1,0:T(8,128)(2,1)S(1)} %get-tuple-element.104), channel_id=1, source_target_pairs={{0,2},{1,3},{4,6},{5,7},{8,10},{9,11},{12,14},{13,15},{16,18},{17,... | collective-permute-start | bytes 688136 | tf_op jit(solution)/shard_map/ppermute | solution.py:899
  46.6 3.6 %query.1 = (bf16[3,4,512,128]{3,2,1,0:T(8,128)(2,1)S(1)}, bf16[3,4,512,128]{3,2,1,0:T(8,128)(2,1)S(1)}, bf16[3,4,512,128]{3,2,1,0:T(8,128)(2,1)S(1)}) custom-call(bf16[3,512,512]{2,1,0:T(8,128)(2,1)S(1)} %get-tuple-element.105.refs_0_.refs_2_, bf16[512,896]{1,0:T(8,128)(2,1)S(1)} %get-tuple-element.106.refs_1_.refs_16_, ...), custom_call_target="tpu_custom_call" | custom-call | flops 345000000 | tf_op jit(solution)/shard_map/query/pallas_call | solution.py:746
  50.2 2.9 %local.1.refs_3_.refs_1_ = f32[3,4,512,128]{3,2,1,0:T(8,128)S(1)} custom-call(bf16[3,4,512,128]{3,2,1,0:T(8,128)(2,1)S(1)} %get-tuple-element.107.refs_0_.refs_2_.refs_5_.refs_3_, bf16[3,4,512,128]{3,2,1,0:T(8,128)(2,1)S(1)} %get-tuple-element.108.refs_1_.refs_4_, bf16[3,4,512,128]{3,2,1,0:T(8,128)(2,1)S(1)} %get-tuple-element.109.refs_2_, ...), custom_call_target="tpu_custom_call" | custom-call | flops 345000000 | tf_op jit(solution)/shard_map/local/pallas_call | solution.py:746
  54.5 4.1 %finish.1 = (f32[3,4,512,128]{3,2,1,0:T(8,128)S(1)}, f32[3,4,512,128]{3,2,1,0:T(8,128)S(1)}, bf16[3,4,2,128,128]{4,3,2,1,0:T(8,128)(2,1)S(1)}, bf16[3,256,256]{2,1,0:T(8,128)(2,1)S(1)}, bf16[3,256,256]{2,1,0:T(8,128)(2,1)S(1)}) custom-call(s32[4]{0:T(128)S(1)} %pad_add_fusion.refs_0_, f32[3,4,512,128]{3,2,1,0:T(8,128)S(1)} %local.1.refs_3_.refs_1_, ...), custom_call_target="tpu_custom_call" | custom-call | flops 345000000 | tf_op jit(solution)/shard_map/finish/pallas_call | solution.py:746
  58.6 4.6 %collective-permute-done.14.refs_0_ = bf16[2,144,512]{2,1,0:T(8,128)(2,1)S(1)} collective-permute-done((bf16[2,144,512]{2,1,0:T(8,128)(2,1)S(1)}, bf16[2,144,512]{2,1,0:T(8,128)(2,1)S(1)}, u32[]{:S(2)}, u32[]{:S(2)}) %collective-permute-start.14) | collective-permute-done | bytes 294944 | tf_op jit(solution)/shard_map/ppermute | solution.py:759
  64.1 2.1 %collective-permute-done.16.refs_2_ = bf16[3,256,256]{2,1,0:T(8,128)(2,1)S(1)} collective-permute-done((bf16[3,256,256]{2,1,0:T(8,128)(2,1)S(1)}, bf16[3,256,256]{2,1,0:T(8,128)(2,1)S(1)}, u32[]{:S(2)}, u32[]{:S(2)}) %collective-permute-start.16) | collective-permute-done | bytes 393248 | tf_op jit(solution)/shard_map/ppermute | solution.py:759
  66.2 7.9 %feed_first.1 = (bf16[2,2,4,128,512]{4,3,2,1,0:T(8,128)(2,1)S(1)}, f32[768,512]{1,0:T(8,128)S(1)}, f32[768,512]{1,0:T(8,128)S(1)}, f32[768,512]{1,0:T(8,128)S(1)...) custom-call(s32[4]{0:T(128)S(1)} %pad_add_fusion.refs_0_, ...), custom_call_target="tpu_custom_call" | custom-call | flops 11500000256 | tf_op jit(solution)/shard_map/feed_first/pallas_call | solution.py:746
  74.3 9.5 %feed_second.1 = (bf16[3,256,512]{2,1,0:T(8,128)(2,1)}, f32[3,256,512]{2,1,0:T(8,128)S(1)}, bf16[3,256,256]{2,1,0:T(8,128)(2,1)S(1)}, bf16[3,256,256]{2,1,0:T(8,...) custom-call(s32[4]{0:T(128)S(1)} %pad_add_fusion.refs_0_, ...), custom_call_target="tpu_custom_call" | custom-call | flops 11500000256 | tf_op jit(solution)/shard_map/feed_second/pallas_call | solution.py:746
  88.3 5.2 %adjoint.1 = (bf16[3,4,512,128]{3,2,1,0:T(8,128)(2,1)S(1)}, bf16[3,4,512,128]{3,2,1,0:T(8,128)(2,1)S(1)}, f32[3,4,128,128]{3,2,1,0:T(8,128)S(1)}, bf16[7,128,128]{2,1,0:T(8,128)(2,1)S(1)}) custom-call(s32[4]{0:T(128)S(1)} %pad_add_fusion.refs_0_, bf16[3,256,256]{2,1,0:T(8,128)(2,1)S(1)} %get-tuple-element.131.refs_1_, ...), custom_call_target="tpu_custom_call" | custom-call | flops 345000000 | tf_op jit(solution)/shard_map/adjoint/pallas_call | solution.py:746
  94.9 5.3 %local_back.1 = (f32[3,4,512,128]{3,2,1,0:T(8,128)S(1)}, f32[3,4,512,128]{3,2,1,0:T(8,128)S(1)}, f32[3,4,512,128]{3,2,1,0:T(8,128)S(1)}) custom-call(bf16[3,4,512,128]{3,2,1,0:T(8,128)(2,1)S(1)} %get-tuple-element.107.refs_0_.refs_2_.refs_5_.refs_3_, bf16[3,4,512,128]{3,2,1,0:T(8,128)(2,1)S(1)} %get-tuple-element.108.refs_1_.refs_4_, ...), custom_call_target="tpu_custom_call" | custom-call | flops 345000000 | tf_op jit(solution)/shard_map/local_back/pallas_call | solution.py:746
  105.4 2.2 %collective-permute-done.22.refs_13_ = bf16[7,128,128]{2,1,0:T(8,128)(2,1)S(1)} collective-permute-done((bf16[7,128,128]{2,1,0:T(8,128)(2,1)S(1)}, bf16[7,128,128]{2,1,0:T(8,128)(2,1)S(1)}, u32[]{:S(2)}, u32[]{:S(2)}) %collective-permute-start.22) | collective-permute-done | bytes 229408 | tf_op jit(solution)/shard_map/ppermute | solution.py:1020
  107.7 12.4 %close.1 = (bf16[4,32,896]{2,1,0:T(8,128)(2,1)S(1)}, bf16[4,32,896]{2,1,0:T(8,128)(2,1)S(1)}, bf16[4,32,896]{2,1,0:T(8,128)(2,1)S(1)}, bf16[4,32,896]{2,1,0:T(8,...) custom-call(s32[4]{0:T(128)S(1)} %pad_add_fusion.refs_0_, f32[3,512,512]{2,1,0:T(8,128)S(1)} %copy-done.7, ...), custom_call_target="tpu_custom_call" | custom-call | flops 16904999936 | tf_op jit(solution)/shard_map/close/pallas_call | solution.py:746
  121.6 2.0 %collective-permute-start.30 = (bf16[4,32,896]{2,1,0:T(8,128)(2,1)S(1)}, bf16[4,32,896]{2,1,0:T(8,128)(2,1)S(1)}, u32[]{:S(2)}, u32[]{:S(2)}) collective-permute-start(bf16[4,32,896]{2,1,0:T(8,128)(2,1)S(1)} %get-tuple-element.164), channel_id=1, source_target_pairs={{0,6},{1,7},{2,4},{3,5},{4,2},{5,3},{6,0},{7,1},{8,14},{9,15},{10,... | collective-permute-start | bytes 688136 | tf_op jit(solution)/shard_map/ppermute | solution.py:759
  127.4 5.1 %collective-permute-done.29.refs_2_ = bf16[4,32,896]{2,1,0:T(8,128)(2,1)S(1)} collective-permute-done((bf16[4,32,896]{2,1,0:T(8,128)(2,1)S(1)}, bf16[4,32,896]{2,1,0:T(8,128)(2,1)S(1)}, u32[]{:S(2)}, u32[]{:S(2)}) %collective-permute-start.29) | collective-permute-done | bytes 229408 | tf_op jit(solution)/shard_map/ppermute | solution.py:759
  132.5 3.0 %collective-permute-start.36 = (bf16[144,512]{1,0:T(8,128)(2,1)S(1)}, bf16[144,512]{1,0:T(8,128)(2,1)S(1)}, u32[]{:S(2)}, u32[]{:S(2)}) collective-permute-start(bf16[144,512]{1,0:T(8,128)(2,1)S(1)} %get-tuple-element.171), channel_id=1, source_target_pairs={{0,24},{1,25},{2,26},{3,27},{4,28},{5,29},{6,30},{7,31},{8,16},{9,... | collective-permute-start | bytes 442376 | tf_op jit(solution)/shard_map/ppermute | solution.py:759
  137.2 3.0 %collective-permute-start.33 = (bf16[32,896]{1,0:T(8,128)(2,1)S(1)}, bf16[32,896]{1,0:T(8,128)(2,1)S(1)}, u32[]{:S(2)}, u32[]{:S(2)}) collective-permute-start(bf16[32,896]{1,0:T(8,128)(2,1)S(1)} %get-tuple-element.168), channel_id=1, source_target_pairs={{0,24},{1,25},{2,26},{3,27},{4,28},{5,29},{6,30},{7,31},{8,16},{9,... | collective-permute-start | bytes 172040 | tf_op jit(solution)/shard_map/ppermute | solution.py:759
  142.1 2.3 %input_grad.1 = (f32[3,256,512]{2,1,0:T(8,128)}, f32[8,128]{1,0:T(8,128)S(1)}) custom-call(bf16[3,256,512]{2,1,0:T(8,128)(2,1)S(1)} %copy-done.2, f32[3,256,512]{2,1,0:T(8,128)S(1)} %get-tuple-element.128.refs_1_, f32[3,256,512]{2,1,0:T(8,128)S(1)} %get-tuple-element.154.refs_4_.refs_2_, bf16[3,256,512]{2,1,0:T(8,128)(2,1)S(1)} %collective-permute-done.25.refs_3_.refs_5_, ...), custom_call_target="tpu_custom_call" | custom-call | flops 345000000 | tf_op jit(solution)/shard_map/input_grad/pallas_call | solution.py:746
  (132 shorter events, 42.5 us)
Async XLA Ops:
  0.7 10.2 %collective-permute-start = (bf16[3,256,512]{2,1,0:T(8,128)(2,1)}, bf16[3,256,512]{2,1,0:T(8,128)(2,1)S(1)}, u32[]{:S(2)}, u32[]{:S(2)}) collective-permute-start(bf16[3,256,512]{2,1,0:T(8,128)(2,1)} %refs_0_.1), channel_id=1, source_target_pairs={{0,1},{1,0},{2,3},{3,2},{4,5},{5,4},{6,7},{7,6},{8,9},{9,8},{10,11... | collective-permute-start | bytes 2359304 | tf_op jit(solution)/shard_map/ppermute | solution.py:759
  5.5 12.1 %collective-permute-start.2 = (bf16[2,16,896]{2,1,0:T(8,128)(2,1)S(1)}, bf16[2,16,896]{2,1,0:T(8,128)(2,1)S(1)}, u32[]{:S(2)}, u32[]{:S(2)}) collective-permute-start(bf16[2,16,896]{2,1,0:T(8,128)(2,1)S(1)} %join.3.refs_1_), channel_id=1, source_target_pairs={{0,8},{1,9},{2,10},{3,11},{4,12},{5,13},{6,14},{7,15},{8,0},{9,1},... | collective-permute-start | bytes 172040 | tf_op jit(solution)/shard_map/ppermute | solution.py:759
  8.3 9.4 %collective-permute-start.3 = (bf16[2,16,896]{2,1,0:T(8,128)(2,1)S(1)}, bf16[2,16,896]{2,1,0:T(8,128)(2,1)S(1)}, u32[]{:S(2)}, u32[]{:S(2)}) collective-permute-start(bf16[2,16,896]{2,1,0:T(8,128)(2,1)S(1)} %join.3.refs_1_), channel_id=1, source_target_pairs={{0,16},{1,17},{2,18},{3,19},{4,20},{5,21},{6,22},{7,23},{8,24},{9,... | collective-permute-start | bytes 172040 | tf_op jit(solution)/shard_map/ppermute | solution.py:759
  18.5 16.7 %collective-permute-start.5 = (bf16[4,2,16,896]{3,2,1,0:T(8,128)(2,1)S(1)}, bf16[4,2,16,896]{3,2,1,0:T(8,128)(2,1)S(1)}, u32[]{:S(2)}, u32[]{:S(2)}) collective-permute-start(bf16[4,2,16,896]{3,2,1,0:T(8,128)(2,1)S(1)} %join.4.refs_2_.refs_5_), channel_id=1, source_target_pairs={{0,4},{1,5},{2,6},{3,7},{4,0},{5,1},{6,2},{7,3},{8,12},{9,13},{10,... | collective-permute-start | bytes 688136 | tf_op jit(solution)/shard_map/ppermute | solution.py:759
  20.1 15.2 %collective-permute-start.6 = (bf16[4,2,16,896]{3,2,1,0:T(8,128)(2,1)S(1)}, bf16[4,2,16,896]{3,2,1,0:T(8,128)(2,1)S(1)}, u32[]{:S(2)}, u32[]{:S(2)}) collective-permute-start(bf16[4,2,16,896]{3,2,1,0:T(8,128)(2,1)S(1)} %join.4.refs_2_.refs_5_), channel_id=1, source_target_pairs={{0,2},{1,3},{2,0},{3,1},{4,6},{5,7},{6,4},{7,5},{8,10},{9,11},{10,... | collective-permute-start | bytes 688136 | tf_op jit(solution)/shard_map/ppermute | solution.py:759
  21.6 13.7 %collective-permute-start.7 = (bf16[4,2,16,896]{3,2,1,0:T(8,128)(2,1)S(1)}, bf16[4,2,16,896]{3,2,1,0:T(8,128)(2,1)S(1)}, u32[]{:S(2)}, u32[]{:S(2)}) collective-permute-start(bf16[4,2,16,896]{3,2,1,0:T(8,128)(2,1)S(1)} %join.4.refs_2_.refs_5_), channel_id=1, source_target_pairs={{0,6},{1,7},{2,4},{3,5},{4,2},{5,3},{6,0},{7,1},{8,14},{9,15},{10,... | collective-permute-start | bytes 688136 | tf_op jit(solution)/shard_map/ppermute | solution.py:759
  32.2 21.0 %collective-permute-start.11 = (bf16[4,144,512]{2,1,0:T(8,128)(2,1)S(1)}, bf16[4,144,512]{2,1,0:T(8,128)(2,1)S(1)}, u32[]{:S(2)}, u32[]{:S(2)}) collective-permute-start(bf16[4,144,512]{2,1,0:T(8,128)(2,1)S(1)} %join.5.refs_0_), channel_id=1, source_target_pairs={{0,4},{1,5},{2,6},{3,7},{4,0},{5,1},{6,2},{7,3},{8,12},{9,13},{10,... | collective-permute-start | bytes 1769480 | tf_op jit(solution)/shard_map/ppermute | solution.py:759
  33.7 19.4 %collective-permute-start.12 = (bf16[4,144,512]{2,1,0:T(8,128)(2,1)S(1)}, bf16[4,144,512]{2,1,0:T(8,128)(2,1)S(1)}, u32[]{:S(2)}, u32[]{:S(2)}) collective-permute-start(bf16[4,144,512]{2,1,0:T(8,128)(2,1)S(1)} %join.5.refs_0_), channel_id=1, source_target_pairs={{0,2},{1,3},{2,0},{3,1},{4,6},{5,7},{6,4},{7,5},{8,10},{9,11},{10,... | collective-permute-start | bytes 1769480 | tf_op jit(solution)/shard_map/ppermute | solution.py:759
  44.2 9.0 %collective-permute-start.13 = (bf16[7,128,128]{2,1,0:T(8,128)(2,1)S(1)}, bf16[7,128,128]{2,1,0:T(8,128)(2,1)S(1)}, u32[]{:S(2)}, u32[]{:S(2)}) collective-permute-start(bf16[7,128,128]{2,1,0:T(8,128)(2,1)S(1)} %get-tuple-element.104), channel_id=1, source_target_pairs={{0,2},{1,3},{4,6},{5,7},{8,10},{9,11},{12,14},{13,15},{16,18},{17,... | collective-permute-start | bytes 688136 | tf_op jit(solution)/shard_map/ppermute | solution.py:899
  53.7 12.5 %collective-permute-start.17 = (bf16[12,144,512]{2,1,0:T(8,128)(2,1)S(1)}, bf16[12,144,512]{2,1,0:T(8,128)(2,1)S(1)}, u32[]{:S(2)}, u32[]{:S(2)}) collective-permute-start(bf16[12,144,512]{2,1,0:T(8,128)(2,1)S(1)} %near.1.refs_8_.refs_7_.refs_4_), channel_id=1, source_target_pairs={{0,1},{1,0},{2,3},{3,2},{4,5},{5,4},{6,7},{7,6},{8,9},{9,8},{10,11... | collective-permute-start | bytes 5308424 | tf_op jit(solution)/shard_map/ppermute | solution.py:759
  53.8 9.4 %collective-permute-start.14 = (bf16[2,144,512]{2,1,0:T(8,128)(2,1)S(1)}, bf16[2,144,512]{2,1,0:T(8,128)(2,1)S(1)}, u32[]{:S(2)}, u32[]{:S(2)}) collective-permute-start(bf16[2,144,512]{2,1,0:T(8,128)(2,1)S(1)} %get-tuple-element.114.refs_3_.refs_7_), channel_id=1, source_target_pairs={{0,2},{1,3},{2,0},{3,1},{4,6},{5,7},{6,4},{7,5},{8,10},{9,11},{10,... | collective-permute-start | bytes 884744 | tf_op jit(solution)/shard_map/ppermute | solution.py:759
  53.9 9.3 %collective-permute-start.15 = (bf16[2,144,512]{2,1,0:T(8,128)(2,1)S(1)}, bf16[2,144,512]{2,1,0:T(8,128)(2,1)S(1)}, u32[]{:S(2)}, u32[]{:S(2)}) collective-permute-start(bf16[2,144,512]{2,1,0:T(8,128)(2,1)S(1)} %get-tuple-element.115), channel_id=1, source_target_pairs={{0,4},{1,5},{2,6},{3,7},{4,0},{5,1},{6,2},{7,3},{8,12},{9,13},{10,... | collective-permute-start | bytes 884744 | tf_op jit(solution)/shard_map/ppermute | solution.py:759
  74.1 11.3 %collective-permute-start.20 = (bf16[2,2,4,128,512]{4,3,2,1,0:T(8,128)(2,1)S(1)}, bf16[2,2,4,128,512]{4,3,2,1,0:T(8,128)(2,1)S(1)}, u32[]{:S(2)}, u32[]{:S(2)}) collective-permute-start(bf16[2,2,4,128,512]{4,3,2,1,0:T(8,128)(2,1)S(1)} %get-tuple-element.136), channel_id=1, source_target_pairs={{0,1},{1,0},{2,3},{3,2},{4,5},{5,4},{6,7},{7,6},{8,9},{9,8},{10,11... | collective-permute-start | bytes 6291464 | tf_op jit(solution)/shard_map/ppermute | solution.py:759
  85.9 15.7 %collective-permute-start.23 = (bf16[2,2,144,512]{3,2,1,0:T(8,128)(2,1)S(1)}, bf16[2,2,144,512]{3,2,1,0:T(8,128)(2,1)S(1)}, u32[]{:S(2)}, u32[]{:S(2)}) collective-permute-start(bf16[2,2,144,512]{3,2,1,0:T(8,128)(2,1)S(1)} %get-tuple-element.150), channel_id=1, source_target_pairs={{0,4},{1,5},{2,6},{3,7},{4,0},{5,1},{6,2},{7,3},{8,12},{9,13},{10,... | collective-permute-start | bytes 1769480 | tf_op jit(solution)/shard_map/ppermute | solution.py:759
  86.5 16.2 %collective-permute-start.24 = (bf16[2,2,144,512]{3,2,1,0:T(8,128)(2,1)S(1)}, bf16[2,2,144,512]{3,2,1,0:T(8,128)(2,1)S(1)}, u32[]{:S(2)}, u32[]{:S(2)}) collective-permute-start(bf16[2,2,144,512]{3,2,1,0:T(8,128)(2,1)S(1)} %get-tuple-element.152), channel_id=1, source_target_pairs={{0,2},{1,3},{2,0},{3,1},{4,6},{5,7},{6,4},{7,5},{8,10},{9,11},{10,... | collective-permute-start | bytes 1769480 | tf_op jit(solution)/shard_map/ppermute | solution.py:759
  93.5 14.2 %collective-permute-start.22 = (bf16[7,128,128]{2,1,0:T(8,128)(2,1)S(1)}, bf16[7,128,128]{2,1,0:T(8,128)(2,1)S(1)}, u32[]{:S(2)}, u32[]{:S(2)}) collective-permute-start(bf16[7,128,128]{2,1,0:T(8,128)(2,1)S(1)} %get-tuple-element.147), channel_id=1, source_target_pairs={{2,0},{3,1},{6,4},{7,5},{10,8},{11,9},{14,12},{15,13},{18,16},{19,... | collective-permute-start | bytes 688136 | tf_op jit(solution)/shard_map/ppermute | solution.py:1020
  103.0 18.6 %collective-permute-start.26 = (bf16[2,144,512]{2,1,0:T(8,128)(2,1)S(1)}, bf16[2,144,512]{2,1,0:T(8,128)(2,1)S(1)}, u32[]{:S(2)}, u32[]{:S(2)}) collective-permute-start(bf16[2,144,512]{2,1,0:T(8,128)(2,1)S(1)} %get-tuple-element.156), channel_id=1, source_target_pairs={{0,2},{1,3},{2,0},{3,1},{4,6},{5,7},{6,4},{7,5},{8,10},{9,11},{10,... | collective-permute-start | bytes 884744 | tf_op jit(solution)/shard_map/ppermute | solution.py:759
  103.9 19.7 %collective-permute-start.27 = (bf16[2,144,512]{2,1,0:T(8,128)(2,1)S(1)}, bf16[2,144,512]{2,1,0:T(8,128)(2,1)S(1)}, u32[]{:S(2)}, u32[]{:S(2)}) collective-permute-start(bf16[2,144,512]{2,1,0:T(8,128)(2,1)S(1)} %get-tuple-element.158), channel_id=1, source_target_pairs={{0,4},{1,5},{2,6},{3,7},{4,0},{5,1},{6,2},{7,3},{8,12},{9,13},{10,... | collective-permute-start | bytes 884744 | tf_op jit(solution)/shard_map/ppermute | solution.py:759
  121.6 10.9 %collective-permute-start.29 = (bf16[4,32,896]{2,1,0:T(8,128)(2,1)S(1)}, bf16[4,32,896]{2,1,0:T(8,128)(2,1)S(1)}, u32[]{:S(2)}, u32[]{:S(2)}) collective-permute-start(bf16[4,32,896]{2,1,0:T(8,128)(2,1)S(1)} %get-tuple-element.163), channel_id=1, source_target_pairs={{0,2},{1,3},{2,0},{3,1},{4,6},{5,7},{6,4},{7,5},{8,10},{9,11},{10,... | collective-permute-start | bytes 688136 | tf_op jit(solution)/shard_map/ppermute | solution.py:759
  121.6 14.0 %collective-permute-start.25 = (bf16[3,256,512]{2,1,0:T(8,128)(2,1)S(1)}, bf16[3,256,512]{2,1,0:T(8,128)(2,1)S(1)}, u32[]{:S(2)}, u32[]{:S(2)}) collective-permute-start(bf16[3,256,512]{2,1,0:T(8,128)(2,1)S(1)} %get-tuple-element.155), channel_id=1, source_target_pairs={{0,1},{1,0},{2,3},{3,2},{4,5},{5,4},{6,7},{7,6},{8,9},{9,8},{10,11... | collective-permute-start | bytes 2359304 | tf_op jit(solution)/shard_map/ppermute | solution.py:759
  121.6 14.0 %collective-permute-start.30 = (bf16[4,32,896]{2,1,0:T(8,128)(2,1)S(1)}, bf16[4,32,896]{2,1,0:T(8,128)(2,1)S(1)}, u32[]{:S(2)}, u32[]{:S(2)}) collective-permute-start(bf16[4,32,896]{2,1,0:T(8,128)(2,1)S(1)} %get-tuple-element.164), channel_id=1, source_target_pairs={{0,6},{1,7},{2,4},{3,5},{4,2},{5,3},{6,0},{7,1},{8,14},{9,15},{10,... | collective-permute-start | bytes 688136 | tf_op jit(solution)/shard_map/ppermute | solution.py:759
  123.8 13.4 %collective-permute-start.34 = (bf16[144,512]{1,0:T(8,128)(2,1)S(1)}, bf16[144,512]{1,0:T(8,128)(2,1)S(1)}, u32[]{:S(2)}, u32[]{:S(2)}) collective-permute-start(bf16[144,512]{1,0:T(8,128)(2,1)S(1)} %get-tuple-element.169), channel_id=1, source_target_pairs={{0,8},{1,9},{2,10},{3,11},{4,12},{5,13},{6,14},{7,15},{8,0},{9,1},... | collective-permute-start | bytes 442376 | tf_op jit(solution)/shard_map/ppermute | solution.py:759
  126.1 15.2 %collective-permute-start.35 = (bf16[144,512]{1,0:T(8,128)(2,1)S(1)}, bf16[144,512]{1,0:T(8,128)(2,1)S(1)}, u32[]{:S(2)}, u32[]{:S(2)}) collective-permute-start(bf16[144,512]{1,0:T(8,128)(2,1)S(1)} %get-tuple-element.170), channel_id=1, source_target_pairs={{0,16},{1,17},{2,18},{3,19},{4,20},{5,21},{6,22},{7,23},{8,24},{9,... | collective-permute-start | bytes 442376 | tf_op jit(solution)/shard_map/ppermute | solution.py:759
  135.8 9.4 %collective-permute-start.32 = (bf16[32,896]{1,0:T(8,128)(2,1)S(1)}, bf16[32,896]{1,0:T(8,128)(2,1)S(1)}, u32[]{:S(2)}, u32[]{:S(2)}) collective-permute-start(bf16[32,896]{1,0:T(8,128)(2,1)S(1)} %get-tuple-element.167), channel_id=1, source_target_pairs={{0,16},{1,17},{2,18},{3,19},{4,20},{5,21},{6,22},{7,23},{8,24},{9,... | collective-permute-start | bytes 172040 | tf_op jit(solution)/shard_map/ppermute | solution.py:759
  (32 other events, 155.0 us)
